TPU v7x, 32 devices: a whole 2x2x4 slice. The times are simulated.
32 devices in a mesh: seq: 4 (over z), head: 8 (over y, x, core).
Axes of the slice: x: 2, y: 2, z: 4, core: 2. Of those that a mesh axis runs over, the one named last changes fastest.
Arguments:
- queries: bfloat16 [1024, 8192], P('seq', 'head'), may hold values from -41 to 41
- keys: bfloat16 [4, 200, 8, 128], P('seq', 'head'), may hold values from -4 to 4
- values: bfloat16 [4, 200, 8, 128], P('seq', 'head'), may hold values from -6 to 6
- cotangent: bfloat16 [1024, 8192], P('seq', 'head'), may hold values from -6 to 6
- mask: int32 [1024, 2], P('seq'), may hold values from 0 to 1, as said below
Outputs:
- attended: bfloat16 [1024, 8192], P('seq', 'head')
- grad_query: bfloat16 [1024, 8192], P('seq', 'head')
- grad_keys: bfloat16 [4, 200, 8, 128], P('seq', 'head')
- grad_values: bfloat16 [4, 200, 8, 128], P('seq', 'head')
Inputs may be any that keep to these rules, and one draw needn't show every extreme that they name: mask[t, 0] is 1 where token t attends to the image of its own block of 256 tokens, mask[t, 1] where it attends to the image of the block before. Within each block the ones of column 0 form a suffix that covers at least the block's second half, the ones of column 1 a prefix that holds the block's first token and at most its first 128 tokens, exactly that many in block 1; column 1 is all 0 on the first block.
All inputs are finite; a program needn't handle non-finite values.
Results may differ from a plain program's by a relative error of at most 0.038.
Values may be sent and summed in bfloat16 or wider, within the bound.
A program may use at most 64 MiB of HBM per device.

v0:
```python
import jax
import jax.numpy as jnp
from jax import lax
from jax.sharding import PartitionSpec as P

KVH = 8
HD = 128


NEGATIVE = -1e30


def passed_along(value, axis, by):
    length = lax.axis_size(axis)
    pairs = [(i, i + by) for i in range(length) if 0 <= i + by < length]
    return lax.ppermute(value, axis, pairs)


def spread_heads(shard, copies):
    return jnp.repeat(jnp.transpose(shard, (1, 0, 2)), copies, axis=0)


def block_forward(query_rows, key_rows, value_rows, keep_mask):
    scores = jnp.einsum(
        "rd,kd->rk", query_rows, key_rows, preferred_element_type=jnp.float32
    ) * HD ** (-0.5)
    scores = jnp.where(keep_mask[:, None] > 0, scores, NEGATIVE)
    highest = jnp.max(scores, axis=1)
    powered = jnp.exp(scores - highest[:, None])
    totals = jnp.sum(powered, axis=1)
    partial_value = jnp.dot(
        powered.astype(jnp.bfloat16), value_rows, preferred_element_type=jnp.float32
    )
    return (scores, highest, totals, partial_value)


def finish_backward(weights, grad_rows, row_delta, query_rows, key_rows, value_rows):
    grad_weights = jnp.einsum(
        "rd,kd->rk", grad_rows, value_rows, preferred_element_type=jnp.float32
    )
    grad_scores = (weights * (grad_weights - row_delta[:, None]) * HD ** (-0.5)).astype(
        jnp.bfloat16
    )
    query_grad = jnp.dot(grad_scores, key_rows, preferred_element_type=jnp.float32)
    key_part = jnp.einsum(
        "rk,rd->kd", grad_scores, query_rows, preferred_element_type=jnp.float32
    ).astype(jnp.bfloat16)
    value_part = jnp.einsum(
        "rk,rd->kd", weights.astype(jnp.bfloat16), grad_rows, preferred_element_type=jnp.float32
    ).astype(jnp.bfloat16)
    return (query_grad, key_part, value_part)


def block_backward(
    scores, highest, totals, live_rows, grad_rows, row_delta, query_rows, key_rows, value_rows
):
    weights = live_rows[:, None] * jnp.exp(scores - highest[:, None]) / totals[:, None]
    return finish_backward(weights, grad_rows, row_delta, query_rows, key_rows, value_rows)


def group_sum(received, groups):
    slot_count, row_count, feature = received.shape
    summed = (
        received.astype(jnp.float32)
        .reshape(groups, slot_count // groups, row_count, feature)
        .sum(axis=1)
    )
    return jnp.transpose(summed, (1, 0, 2))


def per_device(queries, keys, values, cotangent, mask):
    head_devices = lax.axis_size("head")
    copies = head_devices // KVH
    tok_rows = queries.shape[0]
    head_count = queries.shape[1] // HD
    vision_rows = keys.shape[1]
    query_rows = queries.reshape(tok_rows * head_count, HD)
    grad_rows = cotangent.reshape(tok_rows * head_count, HD)
    keep_own = jnp.repeat(mask[:, 0], head_count)
    keep_prev = jnp.repeat(mask[:, 1], head_count)
    live_rows = (keep_own + keep_prev > 0).astype(jnp.float32)
    key_own, value_own = (
        lax.all_to_all(
            spread_heads(keys[0], copies), "head", split_axis=0, concat_axis=1, tiled=True
        ),
        lax.all_to_all(
            spread_heads(values[0], copies), "head", split_axis=0, concat_axis=1, tiled=True
        ),
    )
    key_own = key_own[0]
    value_own = value_own[0]
    key_prev, value_prev = passed_along((key_own, value_own), "seq", 1)
    score_own, peak_own, total_own, partial_own = block_forward(
        query_rows, key_own, value_own, keep_own
    )
    score_prev, peak_prev, total_prev, partial_prev = block_forward(
        query_rows, key_prev, value_prev, keep_prev
    )
    highest = jnp.maximum(peak_own, peak_prev)
    scale_own = jnp.exp(peak_own - highest)
    scale_prev = jnp.exp(peak_prev - highest)
    totals = scale_own * total_own + scale_prev * total_prev
    attended = (
        live_rows[:, None]
        * (scale_own[:, None] * partial_own + scale_prev[:, None] * partial_prev)
        / totals[:, None]
    ).astype(jnp.bfloat16)
    row_delta = jnp.sum(grad_rows.astype(jnp.float32) * attended.astype(jnp.float32), axis=1)
    gq_own, gk_own, gv_own = block_backward(
        score_own, highest, totals, live_rows, grad_rows, row_delta, query_rows, key_own, value_own
    )
    gq_prev, gk_prev, gv_prev = block_backward(
        score_prev,
        highest,
        totals,
        live_rows,
        grad_rows,
        row_delta,
        query_rows,
        key_prev,
        value_prev,
    )
    grad_query = (gq_own + gq_prev).astype(jnp.bfloat16).reshape(tok_rows, head_count * HD)
    second_key, second_value = passed_along((gk_prev, gv_prev), "seq", -1)
    returned = (
        lax.all_to_all(
            gk_own.reshape(head_devices, vision_rows, HD),
            "head",
            split_axis=0,
            concat_axis=0,
            tiled=True,
        ),
        lax.all_to_all(
            gv_own.reshape(head_devices, vision_rows, HD),
            "head",
            split_axis=0,
            concat_axis=0,
            tiled=True,
        ),
        lax.all_to_all(
            second_key.reshape(head_devices, vision_rows, HD),
            "head",
            split_axis=0,
            concat_axis=0,
            tiled=True,
        ),
        lax.all_to_all(
            second_value.reshape(head_devices, vision_rows, HD),
            "head",
            split_axis=0,
            concat_axis=0,
            tiled=True,
        ),
    )
    key_sum = group_sum(returned[0], KVH)
    value_sum = group_sum(returned[1], KVH)
    second_key_sum = group_sum(returned[2], KVH)
    second_value_sum = group_sum(returned[3], KVH)
    grad_keys = key_sum + second_key_sum
    grad_values = value_sum + second_value_sum
    attended = attended.reshape(tok_rows, head_count * HD)
    return (
        attended,
        grad_query,
        grad_keys.astype(jnp.bfloat16)[None],
        grad_values.astype(jnp.bfloat16)[None],
    )


def solution(mesh):
    return jax.shard_map(
        per_device,
        mesh=mesh,
        in_specs=(
            P("seq", "head"),
            P("seq", "head", None, None),
            P("seq", "head", None, None),
            P("seq", "head"),
            P("seq", None),
        ),
        out_specs=(
            P("seq", "head"),
            P("seq", "head"),
            P("seq", "head", None, None),
            P("seq", "head", None, None),
        ),
        check_vma=False,
    )
```

profile of v0, /device:TPU:0, one launch (start us, length us, event | category | flops | bytes accessed | tf_op | source)
XLA Modules:
  0.0 69.1 jit_solution(18366514186324696132)
XLA Ops:
  0.6 0.0 copy-start.2
  0.6 1.5 %copy.28 = bf16[1,25,8,128]{3,1,2,0:T(8,128)(2,1)} copy(bf16[1,25,8,128]{3,2,1,0:T(8,128)(2,1)} %param.6) | data formatting | bytes 102400 | tf_op args[1]
  2.1 5.2 %all-to-all-start = ((bf16[8,25,128]{2,1,0:T(8,128)(2,1)}), bf16[8,25,128]{2,1,0:T(8,128)(2,1)S(1)}, u32[]{:S(2)}, u32[]{:S(2)}) async-start(bf16[8,25,128]{2,1,0:T(8,128)(2,1)} %bitcast.38), calls=%async_computation | async-start | bytes 131072 | tf_op jit(solution)/shard_map/all_to_all | solution.py:83
  7.3 1.4 %copy.27 = bf16[1,25,8,128]{3,1,2,0:T(8,128)(2,1)} copy(bf16[1,25,8,128]{3,2,1,0:T(8,128)(2,1)} %param.7) | data formatting | bytes 102400 | tf_op args[2]
  8.8 3.6 %all-to-all-done = bf16[8,25,128]{2,1,0:T(8,128)(2,1)S(1)} async-done(((bf16[8,25,128]{2,1,0:T(8,128)(2,1)}), bf16[8,25,128]{2,1,0:T(8,128)(2,1)S(1)}, u32[]{:S(2)}, u32[]{:S(2)}) %all-to-all-start) | async-done | bytes 51232 | tf_op jit(solution)/shard_map/all_to_all | solution.py:83
  12.3 3.4 %all-to-all-start.1 = ((bf16[8,25,128]{2,1,0:T(8,128)(2,1)}), bf16[8,25,128]{2,1,0:T(8,128)(2,1)S(1)}, u32[]{:S(2)}, u32[]{:S(2)}) async-start(bf16[8,25,128]{2,1,0:T(8,128)(2,1)} %bitcast.37), calls=%async_computation.1 | async-start | bytes 131072 | tf_op jit(solution)/shard_map/all_to_all | solution.py:86
  15.7 0.8 %compare_reduce_fusion = (pred[256]{0:T(512)(128)(4,1)S(1)}, pred[256]{0:T(512)(128)(4,1)S(1)}, f32[256,1]{0,1:T(1,128)S(1)}) fusion(s32[256,2]{0,1:T(2,128)} %param.9), kind=kLoop, calls=%fused_computation.43 | loop fusion | flops 1280 | bytes 3584 | tf_op jit(solution)/shard_map/gt | solution.py:27
  16.5 1.3 %reshape.127 = bf16[2048,128]{1,0:T(8,128)(2,1)S(1)} reshape(bf16[256,1024]{1,0:T(8,128)(2,1)} %param.5) | data formatting | bytes 1048576 | tf_op jit(solution)/shard_map/reshape | solution.py:77
  17.7 0.1 broadcast_in_dim.50
  17.8 0.1 gt.50
  18.0 0.1 broadcast_in_dim.47
  18.1 0.1 gt.47
  18.2 0.1 broadcast_in_dim.46
  18.3 0.1 convert_element_type.82
  18.4 0.0 copy-done.2
  18.4 0.2 reshape.129
  18.7 0.2 copy.22
  18.9 3.5 %collective-permute-start = (bf16[200,128]{1,0:T(8,128)(2,1)S(1)}, bf16[200,128]{1,0:T(8,128)(2,1)S(1)}, u32[]{:S(2)}, u32[]{:S(2)}) collective-permute-start(bf16[200,128]{1,0:T(8,128)(2,1)S(1)} %squeeze.15), channel_id=1, source_target_pairs={{0,8},{8,16},{16,24},{1,9},{9,17},{17,25},{2,10},{10,18},{18,26},{... | collective-permute-start | bytes 153608 | tf_op jit(solution)/shard_map/ppermute | solution.py:16
  22.4 0.0 all-to-all-done.1
  22.4 4.1 %collective-permute-start.1 = (bf16[200,128]{1,0:T(8,128)(2,1)S(1)}, bf16[200,128]{1,0:T(8,128)(2,1)}, u32[]{:S(2)}, u32[]{:S(2)}) collective-permute-start(bf16[200,128]{1,0:T(8,128)(2,1)S(1)} %squeeze.17), channel_id=1, source_target_pairs={{0,8},{8,16},{16,24},{1,9},{9,17},{17,25},{2,10},{10,18},{18,26},{... | collective-permute-start | bytes 153608 | tf_op jit(solution)/shard_map/ppermute | solution.py:16
  26.5 0.5 fusion.23
  27.0 0.2 fusion.9
  27.3 0.0 collective-permute-done
  27.3 0.0 copy-start.4
  27.3 0.5 fusion.22
  27.8 0.0 copy-start
  27.8 0.2 fusion.11
  28.1 0.5 convolution_convert_fusion.1
  28.6 0.4 copy-done
  29.0 1.1 %convolution_convert_fusion = bf16[200,128]{1,0:T(8,128)(2,1)} fusion(bf16[2048,128]{1,0:T(8,128)(2,1)S(1)} %reshape.129, f32[2048,200]{0,1:T(8,128)S(1)} %get-tuple-element.22, f32[2048]{0:T(1024)S(1)} %get-tuple-element.16, f32[2048]{0:T(1024)S(1)} %get-tuple-element.19, f32[2048]{0:T(1024)S(1)} %convert_element_type.82), kind=kOutput, calls=%fused_computation.23 | convolution fusion | flops 106521600 | bytes 2238464 | tf_op jit(solution)/shard_map/rk,rd->kd/dot_general | solution.py:48
  30.1 0.7 reshape.133
  30.8 4.1 %all-to-all-start.4 = ((bf16[8,25,128]{2,1,0:T(8,128)(2,1)}), bf16[8,25,128]{2,1,0:T(8,128)(2,1)}, u32[]{:S(2)}, u32[]{:S(2)}) async-start(bf16[8,25,128]{2,1,0:T(8,128)(2,1)} %reshape.133), calls=%async_computation.4 | async-start | bytes 131072 | tf_op jit(solution)/shard_map/all_to_all | solution.py:133
  34.9 1.4 %collective-permute-start.3 = (bf16[200,128]{1,0:T(8,128)(2,1)}, bf16[200,128]{1,0:T(8,128)(2,1)}, u32[]{:S(2)}, u32[]{:S(2)}) collective-permute-start(bf16[200,128]{1,0:T(8,128)(2,1)} %convolution_convert_fusion), channel_id=1, source_target_pairs={{8,0},{16,8},{24,16},{9,1},{17,9},{25,17},{10,2},{18,10},{26,18},{... | collective-permute-start | bytes 153608 | tf_op jit(solution)/shard_map/ppermute | solution.py:16
  36.3 0.4 convolution_multiply_fusion.2
  36.8 0.0 collective-permute-done.1
  36.8 2.1 %multiply_reduce_fusion = (f32[2048]{0:T(1024)S(1)}, bf16[2048,128]{0,1:T(8,128)(2,1)}) fusion(bf16[2048,128]{0,1:T(8,128)(2,1)S(1)} %copy.22, f32[2048]{0:T(1024)S(1)} %get-tuple-element.16, f32[2048,128]{0,1:T(8,128)S(1)} %convolution_multiply_fusion.2, f32[2048]{0:T(1024)S(1)} %get-tuple-element.17, f32[2048]{0:T(1024)S(1)} %convert_element_type.82, ...), kind=kOutput, calls=%fused_computation.27 | convolution fusion | flops 108034048 | bytes 3827712 | tf_op jit(solution)/shard_map/dot_general | solution.py:31
  38.9 0.7 fusion.6
  39.6 0.5 fusion.24
  40.1 1.5 %fusion.7 = bf16[2048,200]{0,1:T(8,128)(2,1)S(1)} fusion(bf16[2048,128]{1,0:T(8,128)(2,1)S(1)} %reshape.129, bf16[200,128]{1,0:T(8,128)(2,1)} %collective-permute-done.1, f32[2048]{0:T(1024)S(1)} %get-tuple-element.14, f32[2048]{0:T(1024)S(1)} %get-tuple-element.16, f32[2048,200]{0,1:T(8,128)S(1)} %copy-done.1, f32[2048]{0:T(1024)S(1)} %get-tuple-element.19, ...), kind=kOutput, calls=%fused_computation.11 | convolution fusion | flops 107724800 | bytes 3065856 | tf_op jit(solution)/shard_map/rd,kd->rk/dot_general | solution.py:38
  41.6 0.0 copy-start.5
  41.6 0.4 convolution_convert_fusion.3
  42.0 0.7 reshape.131
  42.6 0.0 all-to-all-done.4
  42.6 4.2 %all-to-all-start.2 = ((bf16[8,25,128]{2,1,0:T(8,128)(2,1)}), bf16[8,25,128]{2,1,0:T(8,128)(2,1)S(1)}, u32[]{:S(2)}, u32[]{:S(2)}) async-start(bf16[8,25,128]{2,1,0:T(8,128)(2,1)} %reshape.131), calls=%async_computation.2 | async-start | bytes 131072 | tf_op jit(solution)/shard_map/all_to_all | solution.py:126
  46.8 0.4 convolution_convert_fusion.2
  47.2 1.3 %collective-permute-start.2 = (bf16[200,128]{1,0:T(8,128)(2,1)S(1)}, bf16[200,128]{1,0:T(8,128)(2,1)S(1)}, u32[]{:S(2)}, u32[]{:S(2)}) collective-permute-start(bf16[200,128]{1,0:T(8,128)(2,1)S(1)} %convolution_convert_fusion.2), channel_id=1, source_target_pairs={{8,0},{16,8},{24,16},{9,1},{17,9},{25,17},{10,2},{18,10},{26,18},{... | collective-permute-start | bytes 153608 | tf_op jit(solution)/shard_map/ppermute | solution.py:16
  48.5 0.0 collective-permute-done.3
  48.5 1.5 %reshape.134 = bf16[8,25,128]{2,1,0:T(8,128)(2,1)} reshape(bf16[200,128]{1,0:T(8,128)(2,1)} %collective-permute-done.3) | data formatting | bytes 102400 | tf_op jit(solution)/shard_map/reshape | solution.py:148
  50.0 1.9 %all-to-all-done.2 = bf16[8,25,128]{2,1,0:T(8,128)(2,1)S(1)} async-done(((bf16[8,25,128]{2,1,0:T(8,128)(2,1)}), bf16[8,25,128]{2,1,0:T(8,128)(2,1)S(1)}, u32[]{:S(2)}, u32[]{:S(2)}) %all-to-all-start.2) | async-done | bytes 51232 | tf_op jit(solution)/shard_map/all_to_all | solution.py:126
  51.8 3.3 %all-to-all-start.5 = ((bf16[8,25,128]{2,1,0:T(8,128)(2,1)}), bf16[8,25,128]{2,1,0:T(8,128)(2,1)S(1)}, u32[]{:S(2)}, u32[]{:S(2)}) async-start(bf16[8,25,128]{2,1,0:T(8,128)(2,1)} %reshape.134), calls=%async_computation.5 | async-start | bytes 131072 | tf_op jit(solution)/shard_map/all_to_all | solution.py:147
  55.2 0.0 copy-start.3
  55.2 0.5 fusion.8
  55.7 1.0 %reshape.130 = bf16[256,1024]{1,0:T(8,128)(2,1)} reshape(bf16[2048,128]{1,0:T(8,128)(2,1)S(1)} %fusion.8) | data formatting | bytes 1048576 | tf_op jit(solution)/shard_map/reshape | solution.py:123
  56.8 0.0 copy-done.3
  56.8 0.3 copy.21
  57.0 1.0 %reshape.128 = bf16[256,1024]{1,0:T(8,128)(2,1)} reshape(bf16[2048,128]{1,0:T(8,128)(2,1)S(1)} %copy.21) | data formatting | bytes 1048576 | tf_op jit(solution)/shard_map/reshape | solution.py:161
  58.1 0.0 collective-permute-done.2
  58.1 0.7 reshape.132
  58.7 1.4 %all-to-all-done.5 = bf16[8,25,128]{2,1,0:T(8,128)(2,1)S(1)} async-done(((bf16[8,25,128]{2,1,0:T(8,128)(2,1)}), bf16[8,25,128]{2,1,0:T(8,128)(2,1)S(1)}, u32[]{:S(2)}, u32[]{:S(2)}) %all-to-all-start.5) | async-done | bytes 51232 | tf_op jit(solution)/shard_map/all_to_all | solution.py:147
  60.1 3.3 %all-to-all-start.3 = ((bf16[8,25,128]{2,1,0:T(8,128)(2,1)}), bf16[8,25,128]{2,1,0:T(8,128)(2,1)S(1)}, u32[]{:S(2)}, u32[]{:S(2)}) async-start(bf16[8,25,128]{2,1,0:T(8,128)(2,1)} %reshape.132), calls=%async_computation.3 | async-start | bytes 131072 | tf_op jit(solution)/shard_map/all_to_all | solution.py:140
  63.5 0.9 %fusion.21 = bf16[1,25,8,128]{3,1,2,0:T(8,128)(2,1)S(1)} fusion(bf16[8,25,128]{2,1,0:T(8,128)(2,1)S(1)} %all-to-all-done.5, bf16[8,25,128]{2,1,0:T(8,128)(2,1)} %all-to-all-done.4), kind=kLoop, calls=%fused_computation.37 | loop fusion | flops 102400 | bytes 153600 | tf_op jit(solution)/shard_map/broadcast_in_dim | solution.py:166
  64.4 0.6 copy.24
  65.0 3.4 %all-to-all-done.3 = bf16[8,25,128]{2,1,0:T(8,128)(2,1)S(1)} async-done(((bf16[8,25,128]{2,1,0:T(8,128)(2,1)}), bf16[8,25,128]{2,1,0:T(8,128)(2,1)S(1)}, u32[]{:S(2)}, u32[]{:S(2)}) %all-to-all-start.3) | async-done | bytes 51232 | tf_op jit(solution)/shard_map/all_to_all | solution.py:140
  68.5 0.6 copy.23
  (8 shorter events, 0.1 us)
Async XLA Ops:
  0.6 17.8 %copy-start.2 = (bf16[256,1024]{1,0:T(8,128)(2,1)S(1)}, bf16[256,1024]{1,0:T(8,128)(2,1)}, u32[]{:S(2)}) copy-start(bf16[256,1024]{1,0:T(8,128)(2,1)} %param.8) | copy-start | bytes 1572868
  2.1 10.2 %all-to-all-start = ((bf16[8,25,128]{2,1,0:T(8,128)(2,1)}), bf16[8,25,128]{2,1,0:T(8,128)(2,1)S(1)}, u32[]{:S(2)}, u32[]{:S(2)}) async-start(bf16[8,25,128]{2,1,0:T(8,128)(2,1)} %bitcast.38), calls=%async_computation | async-start | bytes 131072 | tf_op jit(solution)/shard_map/all_to_all | solution.py:83
  12.3 10.1 %all-to-all-start.1 = ((bf16[8,25,128]{2,1,0:T(8,128)(2,1)}), bf16[8,25,128]{2,1,0:T(8,128)(2,1)S(1)}, u32[]{:S(2)}, u32[]{:S(2)}) async-start(bf16[8,25,128]{2,1,0:T(8,128)(2,1)} %bitcast.37), calls=%async_computation.1 | async-start | bytes 131072 | tf_op jit(solution)/shard_map/all_to_all | solution.py:86
  18.9 8.4 %collective-permute-start = (bf16[200,128]{1,0:T(8,128)(2,1)S(1)}, bf16[200,128]{1,0:T(8,128)(2,1)S(1)}, u32[]{:S(2)}, u32[]{:S(2)}) collective-permute-start(bf16[200,128]{1,0:T(8,128)(2,1)S(1)} %squeeze.15), channel_id=1, source_target_pairs={{0,8},{8,16},{16,24},{1,9},{9,17},{17,25},{2,10},{10,18},{18,26},{... | collective-permute-start | bytes 153608 | tf_op jit(solution)/shard_map/ppermute | solution.py:16
  22.4 14.3 %collective-permute-start.1 = (bf16[200,128]{1,0:T(8,128)(2,1)S(1)}, bf16[200,128]{1,0:T(8,128)(2,1)}, u32[]{:S(2)}, u32[]{:S(2)}) collective-permute-start(bf16[200,128]{1,0:T(8,128)(2,1)S(1)} %squeeze.17), channel_id=1, source_target_pairs={{0,8},{8,16},{16,24},{1,9},{9,17},{17,25},{2,10},{10,18},{18,26},{... | collective-permute-start | bytes 153608 | tf_op jit(solution)/shard_map/ppermute | solution.py:16
  27.3 0.8 %copy-start.4 = (bf16[200,128]{1,0:T(8,128)(2,1)}, bf16[200,128]{1,0:T(8,128)(2,1)S(1)}, u32[]{:S(2)}) copy-start(bf16[200,128]{1,0:T(8,128)(2,1)S(1)} %collective-permute-done) | copy-start | bytes 153604
  27.8 1.2 %copy-start = (f32[2048,200]{0,1:T(8,128)}, f32[2048,200]{0,1:T(8,128)S(1)}, u32[]{:S(2)}) copy-start(f32[2048,200]{0,1:T(8,128)S(1)} %get-tuple-element.22) | copy-start | bytes 4915204
  30.8 11.8 %all-to-all-start.4 = ((bf16[8,25,128]{2,1,0:T(8,128)(2,1)}), bf16[8,25,128]{2,1,0:T(8,128)(2,1)}, u32[]{:S(2)}, u32[]{:S(2)}) async-start(bf16[8,25,128]{2,1,0:T(8,128)(2,1)} %reshape.133), calls=%async_computation.4 | async-start | bytes 131072 | tf_op jit(solution)/shard_map/all_to_all | solution.py:133
  34.9 1.9 %copy-start.1 = (f32[2048,200]{0,1:T(8,128)S(1)}, f32[2048,200]{0,1:T(8,128)}, u32[]{:S(2)}) copy-start(f32[2048,200]{0,1:T(8,128)} %copy-done) | copy-start | bytes 4915204
  34.9 13.6 %collective-permute-start.3 = (bf16[200,128]{1,0:T(8,128)(2,1)}, bf16[200,128]{1,0:T(8,128)(2,1)}, u32[]{:S(2)}, u32[]{:S(2)}) collective-permute-start(bf16[200,128]{1,0:T(8,128)(2,1)} %convolution_convert_fusion), channel_id=1, source_target_pairs={{8,0},{16,8},{24,16},{9,1},{17,9},{25,17},{10,2},{18,10},{26,18},{... | collective-permute-start | bytes 153608 | tf_op jit(solution)/shard_map/ppermute | solution.py:16
  41.6 13.6 %copy-start.5 = (bf16[200,128]{1,0:T(8,128)(2,1)S(1)}, bf16[200,128]{1,0:T(8,128)(2,1)}, u32[]{:S(2)}) copy-start(bf16[200,128]{1,0:T(8,128)(2,1)} %copy-done.4) | copy-start | bytes 153604
  42.6 9.2 %all-to-all-start.2 = ((bf16[8,25,128]{2,1,0:T(8,128)(2,1)}), bf16[8,25,128]{2,1,0:T(8,128)(2,1)S(1)}, u32[]{:S(2)}, u32[]{:S(2)}) async-start(bf16[8,25,128]{2,1,0:T(8,128)(2,1)} %reshape.131), calls=%async_computation.2 | async-start | bytes 131072 | tf_op jit(solution)/shard_map/all_to_all | solution.py:126
  47.2 10.9 %collective-permute-start.2 = (bf16[200,128]{1,0:T(8,128)(2,1)S(1)}, bf16[200,128]{1,0:T(8,128)(2,1)S(1)}, u32[]{:S(2)}, u32[]{:S(2)}) collective-permute-start(bf16[200,128]{1,0:T(8,128)(2,1)S(1)} %convolution_convert_fusion.2), channel_id=1, source_target_pairs={{8,0},{16,8},{24,16},{9,1},{17,9},{25,17},{10,2},{18,10},{26,18},{... | collective-permute-start | bytes 153608 | tf_op jit(solution)/shard_map/ppermute | solution.py:16
  51.8 8.3 %all-to-all-start.5 = ((bf16[8,25,128]{2,1,0:T(8,128)(2,1)}), bf16[8,25,128]{2,1,0:T(8,128)(2,1)S(1)}, u32[]{:S(2)}, u32[]{:S(2)}) async-start(bf16[8,25,128]{2,1,0:T(8,128)(2,1)} %reshape.134), calls=%async_computation.5 | async-start | bytes 131072 | tf_op jit(solution)/shard_map/all_to_all | solution.py:147
  55.2 1.6 %copy-start.3 = (bf16[2048,128]{0,1:T(8,128)(2,1)S(1)}, bf16[2048,128]{0,1:T(8,128)(2,1)}, u32[]{:S(2)}) copy-start(bf16[2048,128]{0,1:T(8,128)(2,1)} %get-tuple-element.15) | copy-start | bytes 1572868
  60.1 8.3 %all-to-all-start.3 = ((bf16[8,25,128]{2,1,0:T(8,128)(2,1)}), bf16[8,25,128]{2,1,0:T(8,128)(2,1)S(1)}, u32[]{:S(2)}, u32[]{:S(2)}) async-start(bf16[8,25,128]{2,1,0:T(8,128)(2,1)} %reshape.132), calls=%async_computation.3 | async-start | bytes 131072 | tf_op jit(solution)/shard_map/all_to_all | solution.py:140
where the time goes:
time: 70.1 us; the launch traced here: 69.1 us
  starting transfers between devices  33.8 us (48%)
  local copies, waits for them, and re-layouts  12.8 us (18%)
  waiting for transfers between devices  10.3 us (15%)
  matrix products  9.04 us (13%)
  other arithmetic  2.16 us (3%)
  between operations  0.93 us (1%)
    ppermute x4, starting transfers between devices, passed_along(): return lax.ppermute(value, axis, pairs)  10.3 us
    all_to_all x1, starting transfers between devices, per_device(): lax.all_to_all(spread_heads(keys[0], copies), 'head', split_axis=0, conca...  5.17 us
    unnamed x16, local copies, waits for them, and re-layouts  4.66 us
    all_to_all x1, starting transfers between devices, per_device(): lax.all_to_all(gk_own.reshape(head_devices, vision_rows, HD), 'head', spl...  4.19 us
    all_to_all x1, starting transfers between devices, per_device(): lax.all_to_all(gv_own.reshape(head_devices, vision_rows, HD), 'head', spl...  4.13 us
    all_to_all x1, waiting for transfers between devices, per_device(): lax.all_to_all(spread_heads(keys[0], copies), 'head', split_axis=0, conca...  3.57 us
    all_to_all x1, waiting for transfers between devices, per_device(): lax.all_to_all(second_key.reshape(head_devices, vision_rows, HD), 'head',...  3.44 us
    all_to_all x1, starting transfers between devices, per_device(): lax.all_to_all(spread_heads(values[0], copies), 'head', split_axis=0, con...  3.35 us
  transfers between devices with their start and end apart: 10, of which 4 were waited for; matrix products, arithmetic and copies ran while one was open for 31% of the time, Pallas kernels for 0%

commit v1 on v0

v1 whole, which is shorter than its diff:
```python
import functools
import math

import jax
import jax.numpy as jnp
from jax import lax
from jax.experimental import pallas as pl
from jax.experimental.pallas import tpu as pltpu
from jax.sharding import PartitionSpec as P

KVH = 8
HD = 128
NEGATIVE = -1e30
MESH = pl.DeviceIdType.MESH
SCALE = HD ** -0.5
EXP2_SCALE = SCALE * math.log2(math.e)


def dot(a, b):
    return jnp.dot(a, b, preferred_element_type=jnp.float32)


def dot_nt(a, b):
    return lax.dot_general(a, b, (((1,), (1,)), ((), ())), preferred_element_type=jnp.float32)


def each(count, body):
    if count <= 8:
        for i in range(count):
            body(i)
    else:
        lax.fori_loop(0, count, lambda i, c: (body(i), c)[1], 0)


def slot_map(pad, vision, transposed):
    shape = (vision * KVH, KVH * pad) if transposed else (KVH * pad, vision * KVH)
    slot = lax.broadcasted_iota(jnp.int32, shape, 1 if transposed else 0)
    row = lax.broadcasted_iota(jnp.int32, shape, 0 if transposed else 1)
    head, token = slot // pad, slot % pad
    return jnp.where((token < vision) & (row == token * KVH + head), 1.0, 0.0).astype(jnp.bfloat16)


def kernel(
    n_seq, n, pad, vision, group,
    q_hbm, k_ref, v_ref, do_hbm, mask_ref,
    att_hbm, gq_hbm, gk_ref, gv_ref,
    q, do, att, gq, qt, dot_t, stage, kv, part, ret, bias,
    in_sem, out_sem, kv_send, kv_recv, part_send, part_recv,
):
    s = lax.axis_index("seq")
    me = lax.axis_index("head")
    copies = n // KVH
    tokens, width = q.shape
    heads = width // HD
    half = tokens // 2
    cols = n * pad
    not_first = s > 0
    not_last = s < n_seq - 1

    loads = []
    for i, rows in enumerate((pl.ds(half, half), pl.ds(0, half))):
        for k, (src, dst) in enumerate(((q_hbm, q), (do_hbm, do))):
            load = pltpu.make_async_copy(src.at[rows], dst.at[rows], in_sem.at[i, k])
            load.start()
            loads.append(load)

    barrier = pltpu.get_barrier_semaphore()

    def greet(block, peer):
        pl.semaphore_signal(
            barrier, inc=1, device_id={"seq": block, "head": peer}, device_id_type=MESH
        )

    each(n - 1, lambda i: greet(s, lax.rem(me + 1 + i, n)))

    @pl.when(not_first)
    def _():
        each(n, lambda i: greet(s - 1, lax.rem(me + i, n)))

    @pl.when(not_last)
    def _():
        each(n, lambda i: greet(s + 1, lax.rem(me + i, n)))

    spread = slot_map(pad, vision, False)
    stage[:, :HD] = dot(spread, k_ref[...]).astype(jnp.bfloat16)
    stage[:, HD:] = dot(spread, v_ref[...]).astype(jnp.bfloat16)

    def rows_of(index):
        return pl.ds(pl.multiple_of(index * pad, pad), pad)

    def kv_copy(b, block, peer, source):
        return pltpu.make_async_remote_copy(
            src_ref=stage.at[rows_of(peer // copies)],
            dst_ref=kv.at[b, rows_of(source)],
            send_sem=kv_send.at[b, peer],
            recv_sem=kv_recv.at[b, source],
            device_id={"seq": block, "head": peer},
            device_id_type=MESH,
        )

    def part_copy(b, block, peer, source):
        return pltpu.make_async_remote_copy(
            src_ref=part.at[b, rows_of(peer)],
            dst_ref=ret.at[b, rows_of(source)],
            send_sem=part_send.at[b, peer],
            recv_sem=part_recv.at[b, source],
            device_id={"seq": block, "head": peer},
            device_id_type=MESH,
        )

    pl.semaphore_wait(
        barrier, (n - 1) + n * not_first.astype(jnp.int32) + n * not_last.astype(jnp.int32)
    )

    each(n - 1, lambda i: kv_copy(0, s, lax.rem(me + 1 + i, n), me).start())

    @pl.when(not_last)
    def _():
        each(n, lambda i: kv_copy(1, s + 1, lax.rem(me + i, n), me).start())

    kv[0, rows_of(me), :] = stage[rows_of(me // copies), :]

    @pl.when(s == 0)
    def _():
        kv[1] = jnp.zeros(kv.shape[1:], kv.dtype)

    @pl.when(s == n_seq - 1)
    def _():
        ret[1] = jnp.zeros(ret.shape[1:], ret.dtype)

    slot_col = lax.broadcasted_iota(jnp.int32, (half, cols), 1)
    used = slot_col % pad < vision
    keep_own = mask_ref[:half, 0:1]
    keep_prev = mask_ref[:half, 1:2]
    bias[:, :cols] = jnp.where(used & (keep_own > 0), 0.0, NEGATIVE)
    bias[:, cols:] = jnp.where(used & (keep_prev > 0), 0.0, NEGATIVE)
    live = (keep_own + keep_prev > 0).astype(jnp.float32)
    live = jnp.concatenate([live] * group, axis=0)
    own_bias = jnp.where(used[:1], 0.0, NEGATIVE)

    for load in loads:
        load.wait()
    for h in range(heads):
        at = slice(h * HD, (h + 1) * HD)
        for b in range(2):
            to = slice(h * half, (h + 1) * half)
            rows = slice(b * half, (b + 1) * half)
            qt[b, :, to] = q[rows, at].T
            dot_t[b, :, to] = do[rows, at].T

    def stacked(ref, rows, first):
        return jnp.concatenate(
            [ref[rows, (first + i) * HD:(first + i + 1) * HD] for i in range(group)], axis=0
        )

    def attend(rows, b, first, keys, values, score_bias, live_rows):
        query = stacked(q, rows, first)
        grad = stacked(do, rows, first)
        scores = dot_nt(query, keys) + score_bias
        peak = jnp.max(scores, axis=1, keepdims=True)
        powered = jnp.exp2((scores - peak) * EXP2_SCALE)
        weights = powered * (live_rows / jnp.sum(powered, axis=1, keepdims=True))
        rounded = weights.astype(jnp.bfloat16)
        attended = dot(rounded, values)
        delta = jnp.sum(grad.astype(jnp.float32) * attended, axis=1, keepdims=True)
        grad_weights = dot_nt(grad, values)
        grad_scores = (weights * (grad_weights - delta)).astype(jnp.bfloat16)
        grad_query = dot(grad_scores, keys) * SCALE
        for i in range(group):
            at = slice((first + i) * HD, (first + i + 1) * HD)
            att[rows, at] = attended[i * half:(i + 1) * half].astype(jnp.bfloat16)
            gq[rows, at] = grad_query[i * half:(i + 1) * half].astype(jnp.bfloat16)
        to = slice(first * half, (first + group) * half)
        return dot(qt[b, :, to], grad_scores), dot(dot_t[b, :, to], rounded)

    def put(b, key_sum, value_sum):
        part[b, :, :HD] = (key_sum * SCALE).T.astype(jnp.bfloat16)
        part[b, :, HD:] = value_sum.T.astype(jnp.bfloat16)

    def write_out(b):
        rows = pl.ds(b * half, half)
        stores = [
            pltpu.make_async_copy(att.at[rows], att_hbm.at[rows], out_sem.at[b, 0]),
            pltpu.make_async_copy(gq.at[rows], gq_hbm.at[rows], out_sem.at[b, 1]),
        ]
        for store in stores:
            store.start()
        return stores

    upper, lower = slice(half, tokens), slice(0, half)
    firsts = list(range(0, heads, group))
    cut = len(firsts) // 2

    each(n - 1, lambda i: kv_copy(0, s, me, lax.rem(me + 1 + i, n)).wait_recv())
    key_sum, value_sum = 0.0, 0.0
    keys, values = kv[0, :, :HD], kv[0, :, HD:]
    for first in firsts[:cut]:
        key_term, value_term = attend(upper, 1, first, keys, values, own_bias, 1.0)
        key_sum, value_sum = key_sum + key_term, value_sum + value_term

    @pl.when(not_first)
    def _():
        each(n, lambda i: kv_copy(1, s, me, lax.rem(me + i, n)).wait_recv())

    both_keys = kv[:, :, :HD].reshape(2 * cols, HD)
    both_values = kv[:, :, HD:].reshape(2 * cols, HD)
    both_bias = jnp.concatenate([bias[...]] * group, axis=0)
    key_both, value_both = 0.0, 0.0
    for first in firsts:
        key_term, value_term = attend(lower, 0, first, both_keys, both_values, both_bias, live)
        key_both, value_both = key_both + key_term, value_both + value_term
    put(1, key_both[:, cols:], value_both[:, cols:])

    @pl.when(not_first)
    def _():
        each(n, lambda i: part_copy(1, s - 1, lax.rem(me + i, n), me).start())

    stores = write_out(0)
    key_sum, value_sum = key_sum + key_both[:, :cols], value_sum + value_both[:, :cols]
    for first in firsts[cut:]:
        key_term, value_term = attend(upper, 1, first, keys, values, own_bias, 1.0)
        key_sum, value_sum = key_sum + key_term, value_sum + value_term
    put(0, key_sum, value_sum)
    each(n - 1, lambda i: part_copy(0, s, lax.rem(me + 1 + i, n), me).start())
    stores += write_out(1)
    ret[0, rows_of(me), :] = part[0, rows_of(me), :]

    gather = slot_map(pad, vision, True)
    each(n - 1, lambda i: part_copy(0, s, me, lax.rem(me + 1 + i, n)).wait_recv())

    @pl.when(not_last)
    def _():
        each(n, lambda i: part_copy(1, s, me, lax.rem(me + i, n)).wait_recv())

    total = ret[0].astype(jnp.float32) + ret[1].astype(jnp.float32)
    total = total.reshape(KVH, copies, pad, 2 * HD).sum(axis=1).reshape(KVH * pad, 2 * HD)
    grads = dot(gather, total.astype(jnp.bfloat16)).astype(jnp.bfloat16)
    gk_ref[...] = grads[:, :HD]
    gv_ref[...] = grads[:, HD:]

    each(n - 1, lambda i: kv_copy(0, s, lax.rem(me + 1 + i, n), me).wait_send())
    each(n - 1, lambda i: part_copy(0, s, lax.rem(me + 1 + i, n), me).wait_send())

    @pl.when(not_last)
    def _():
        each(n, lambda i: kv_copy(1, s + 1, lax.rem(me + i, n), me).wait_send())

    @pl.when(not_first)
    def _():
        each(n, lambda i: part_copy(1, s - 1, lax.rem(me + i, n), me).wait_send())

    for store in stores:
        store.wait()


def per_device(n_seq, n, queries, keys, values, cotangent, mask):
    tokens, width = queries.shape
    vision = keys.shape[1]
    pad = -(-vision // 16) * 16
    heads = width // HD
    group = min(2, heads)
    half = tokens // 2
    cols = n * pad
    bf16, f32 = jnp.bfloat16, jnp.float32
    vmem = pl.BlockSpec(memory_space=pltpu.VMEM)
    hbm = pl.BlockSpec(memory_space=pl.ANY)
    dma = pltpu.SemaphoreType.DMA
    attended, grad_query, grad_keys, grad_values = pl.pallas_call(
        functools.partial(kernel, n_seq, n, pad, vision, group),
        out_shape=(
            jax.ShapeDtypeStruct((tokens, width), bf16),
            jax.ShapeDtypeStruct((tokens, width), bf16),
            jax.ShapeDtypeStruct((vision * KVH, HD), bf16),
            jax.ShapeDtypeStruct((vision * KVH, HD), bf16),
        ),
        in_specs=[hbm, vmem, vmem, hbm, vmem],
        out_specs=(hbm, hbm, vmem, vmem),
        scratch_shapes=[
            pltpu.VMEM((tokens, width), bf16),
            pltpu.VMEM((tokens, width), bf16),
            pltpu.VMEM((tokens, width), bf16),
            pltpu.VMEM((tokens, width), bf16),
            pltpu.VMEM((2, HD, heads * half), bf16),
            pltpu.VMEM((2, HD, heads * half), bf16),
            pltpu.VMEM((KVH * pad, 2 * HD), bf16),
            pltpu.VMEM((2, cols, 2 * HD), bf16),
            pltpu.VMEM((2, cols, 2 * HD), bf16),
            pltpu.VMEM((2, cols, 2 * HD), bf16),
            pltpu.VMEM((half, 2 * cols), f32),
            dma((2, 2)),
            dma((2, 2)),
            dma((2, n)),
            dma((2, n)),
            dma((2, n)),
            dma((2, n)),
        ],
        compiler_params=pltpu.CompilerParams(
            collective_id=0, has_side_effects=True, vmem_limit_bytes=48 * 1024 * 1024
        ),
    )(
        queries,
        keys.reshape(vision * KVH, HD),
        values.reshape(vision * KVH, HD),
        cotangent,
        mask,
    )
    shape = (1, vision, KVH, HD)
    return attended, grad_query, grad_keys.reshape(shape), grad_values.reshape(shape)


def solution(mesh):
    return jax.shard_map(
        functools.partial(per_device, mesh.shape["seq"], mesh.shape["head"]),
        mesh=mesh,
        in_specs=(
            P("seq", "head"),
            P("seq", "head", None, None),
            P("seq", "head", None, None),
            P("seq", "head"),
            P("seq", None),
        ),
        out_specs=(
            P("seq", "head"),
            P("seq", "head"),
            P("seq", "head", None, None),
            P("seq", "head", None, None),
        ),
        check_vma=False,
    )
```

time: 70.1 us -> 27.9 us (0.40); the launches traced: 69.1 us -> 27.7 us
  starting transfers between devices: 33.8 us -> 0 us
  Pallas kernels: 0 us -> 20.6 us
  waiting for transfers between devices: 10.3 us -> 0 us
  matrix products: 9.04 us -> 0 us
  local copies, waits for them, and re-layouts: 12.8 us -> 6.41 us
  other arithmetic: 2.16 us -> 0 us
    all_to_all x6 -> x0, starting transfers between devices: 23.5 us -> none  [the longest x1 5.17 us: per_device(): lax.all_to_all(spread_heads(keys[0], copies), 'head', split_axis=0, conca...]
    pallas_call x0 -> x1, Pallas kernels: none -> 20.6 us  [per_device(): pl.pallas_call(functools.partial(kernel, n_seq, n, pad, vision, group), o...]
    all_to_all x6 -> x0, waiting for transfers between devices: 10.3 us -> none  [the longest x1 3.57 us: per_device(): lax.all_to_all(spread_heads(keys[0], copies), 'head', split_axis=0, conca...]
    ppermute x4 -> x0, starting transfers between devices: 10.3 us -> none  [passed_along(): return lax.ppermute(value, axis, pairs)]
    dot_general x12 -> x0, matrix products: 9.04 us -> none  [the longest x2 2.56 us: block_forward(): jnp.dot(powered.astype(jnp.bfloat16), value_rows, preferred_element_type=...]
    reshape x9 -> x0, local copies, waits for them, and re-layouts: 7.18 us -> none  [the longest x1 1.46 us: per_device(): second_value.reshape(head_devices, vision_rows, HD)]
    unnamed x16 -> x15, local copies, waits for them, and re-layouts: 4.66 us -> 6.41 us
    broadcast_in_dim x2 -> x0, other arithmetic: 0.88 us -> none  [the longest x1 0.86 us: per_device(): grad_values.astype(jnp.bfloat16)[None]]
  transfers between devices with their start and end apart: 10 -> 0, of which waited for: 4 -> 0; matrix products, arithmetic and copies ran while one was open for 31% -> 0% of each run, Pallas kernels for 0% -> 0%
where the time goes in v1:
time: 27.9 us; the launch traced here: 27.7 us
  Pallas kernels  20.6 us (74%)
  local copies, waits for them, and re-layouts  6.41 us (23%)
  between operations  0.66 us (2%)
    pallas_call x1, Pallas kernels, per_device(): pl.pallas_call(functools.partial(kernel, n_seq, n, pad, vision, group), o...  20.6 us
    unnamed x15, local copies, waits for them, and re-layouts  6.41 us

profile of v1, /device:TPU:0, one launch (start us, length us, event | category | flops | bytes accessed | tf_op | source)
XLA Modules:
  0.0 27.7 jit_solution(3721915419047899889)
XLA Ops:
  0.6 0.0 copy-start.4
  0.6 0.7 %copy-done.4 = s32[256,2]{0,1:T(2,128)S(1)} copy-done((s32[256,2]{0,1:T(2,128)S(1)}, s32[256,2]{0,1:T(2,128)}, u32[]{:S(2)}) %copy-start.4) | copy-done | bytes 2072
  1.3 0.0 copy-start.2
  1.3 0.0 copy-start.3
  1.3 0.1 copy.9.mask_ref
  1.5 0.7 %copy-done.2 = bf16[1,25,8,128]{3,2,1,0:T(8,128)(2,1)S(1)} copy-done((bf16[1,25,8,128]{3,2,1,0:T(8,128)(2,1)S(1)}, bf16[1,25,8,128]{3,2,1,0:T(8,128)(2,1)}, u32[]{:S(2)}) %copy-start.2) | copy-done | bytes 51224
  2.1 0.0 copy-done.3
  2.1 0.0 copy-start
  2.1 1.0 %copy-done = bf16[256,1024]{1,0:T(8,128)(2,1)S(1)} copy-done((bf16[256,1024]{1,0:T(8,128)(2,1)S(1)}, bf16[256,1024]{1,0:T(8,128)(2,1)}, u32[]{:S(2)}) %copy-start) | copy-done | bytes 524312
  3.2 0.0 copy-start.1
  3.2 1.0 %copy-done.1 = bf16[256,1024]{1,0:T(8,128)(2,1)S(1)} copy-done((bf16[256,1024]{1,0:T(8,128)(2,1)S(1)}, bf16[256,1024]{1,0:T(8,128)(2,1)}, u32[]{:S(2)}) %copy-start.1) | copy-done | bytes 524312
  4.2 20.6 %shard_map.84 = (bf16[256,1024]{1,0:T(8,128)(2,1)S(1)}, bf16[256,1024]{1,0:T(8,128)(2,1)S(1)}, bf16[200,128]{1,0:T(8,128)(2,1)S(1)}, bf16[200,128]{1,0:T(8,128)(2,1)S(1)}) custom-call(bf16[256,1024]{1,0:T(8,128)(2,1)S(1)} %copy-done, bf16[200,128]{1,0:T(8,128)(2,1)S(1)} %bitcast.6, bf16[200,128]{1,0:T(8,128)(2,1)S(1)} %bitcast.7, ...), custom_call_target="tpu_custom_call" | custom-call | tf_op jit(solution)/shard_map/pallas_call | solution.py:268
  24.8 0.8 %copy.14 = bf16[256,1024]{1,0:T(8,128)(2,1)} copy(bf16[256,1024]{1,0:T(8,128)(2,1)S(1)} %get-tuple-element.16) | data formatting | bytes 1048576
  25.6 0.8 %copy.15 = bf16[256,1024]{1,0:T(8,128)(2,1)} copy(bf16[256,1024]{1,0:T(8,128)(2,1)S(1)} %get-tuple-element.17) | data formatting | bytes 1048576
  26.4 0.6 %copy.16 = bf16[1,25,8,128]{3,2,1,0:T(8,128)(2,1)} copy(bf16[1,25,8,128]{3,2,1,0:T(8,128)(2,1)S(1)} %bitcast.5) | data formatting | bytes 102400
  27.0 0.6 %copy.17 = bf16[1,25,8,128]{3,2,1,0:T(8,128)(2,1)} copy(bf16[1,25,8,128]{3,2,1,0:T(8,128)(2,1)S(1)} %bitcast.4) | data formatting | bytes 102400
Async XLA Ops:
  0.6 0.7 %copy-start.4 = (s32[256,2]{0,1:T(2,128)S(1)}, s32[256,2]{0,1:T(2,128)}, u32[]{:S(2)}) copy-start(s32[256,2]{0,1:T(2,128)} %param.9) | copy-start | bytes 6148
  1.3 0.8 %copy-start.2 = (bf16[1,25,8,128]{3,2,1,0:T(8,128)(2,1)S(1)}, bf16[1,25,8,128]{3,2,1,0:T(8,128)(2,1)}, u32[]{:S(2)}) copy-start(bf16[1,25,8,128]{3,2,1,0:T(8,128)(2,1)} %param.6) | copy-start | bytes 153604
  1.3 0.8 %copy-start.3 = (bf16[1,25,8,128]{3,2,1,0:T(8,128)(2,1)S(1)}, bf16[1,25,8,128]{3,2,1,0:T(8,128)(2,1)}, u32[]{:S(2)}) copy-start(bf16[1,25,8,128]{3,2,1,0:T(8,128)(2,1)} %param.7) | copy-start | bytes 153604
  2.1 1.0 %copy-start = (bf16[256,1024]{1,0:T(8,128)(2,1)S(1)}, bf16[256,1024]{1,0:T(8,128)(2,1)}, u32[]{:S(2)}) copy-start(bf16[256,1024]{1,0:T(8,128)(2,1)} %q_hbm.1) | copy-start | bytes 1572868
  3.2 1.0 %copy-start.1 = (bf16[256,1024]{1,0:T(8,128)(2,1)S(1)}, bf16[256,1024]{1,0:T(8,128)(2,1)}, u32[]{:S(2)}) copy-start(bf16[256,1024]{1,0:T(8,128)(2,1)} %do_hbm.1) | copy-start | bytes 1572868

commit v2 on v1

--- a/solution.py
+++ b/solution.py
@@ -11,6 +11,7 @@
 KVH = 8
 HD = 128
 NEGATIVE = -1e30
+VMEM_LIMIT = 58 * 1024 * 1024
 MESH = pl.DeviceIdType.MESH
 SCALE = HD ** -0.5
 EXP2_SCALE = SCALE * math.log2(math.e)
@@ -42,10 +43,10 @@
 
 def kernel(
     n_seq, n, pad, vision, group,
-    q_hbm, k_ref, v_ref, do_hbm, mask_ref,
+    q_hbm, k_hbm, v_hbm, do_hbm, mask_hbm,
     att_hbm, gq_hbm, gk_ref, gv_ref,
-    q, do, att, gq, qt, dot_t, stage, kv, part, ret, bias,
-    in_sem, out_sem, kv_send, kv_recv, part_send, part_recv,
+    q, do, att, gq, k_own, v_own, mask, qt, dot_t, stage, kv, part, ret, bias, gs_lower, gs_upper,
+    in_sem, out_sem, small_sem, kv_send, kv_recv, part_send, part_recv,
 ):
     s = lax.axis_index("seq")
     me = lax.axis_index("head")
@@ -57,6 +58,11 @@
     not_first = s > 0
     not_last = s < n_seq - 1
 
+    small = []
+    for i, (src, dst) in enumerate(((k_hbm, k_own), (v_hbm, v_own), (mask_hbm, mask))):
+        load = pltpu.make_async_copy(src, dst, small_sem.at[i])
+        load.start()
+        small.append(load)
     loads = []
     for i, rows in enumerate((pl.ds(half, half), pl.ds(0, half))):
         for k, (src, dst) in enumerate(((q_hbm, q), (do_hbm, do))):
@@ -81,9 +87,11 @@
     def _():
         each(n, lambda i: greet(s + 1, lax.rem(me + i, n)))
 
+    for load in small:
+        load.wait()
     spread = slot_map(pad, vision, False)
-    stage[:, :HD] = dot(spread, k_ref[...]).astype(jnp.bfloat16)
-    stage[:, HD:] = dot(spread, v_ref[...]).astype(jnp.bfloat16)
+    stage[:, :HD] = dot(spread, k_own[...]).astype(jnp.bfloat16)
+    stage[:, HD:] = dot(spread, v_own[...]).astype(jnp.bfloat16)
 
     def rows_of(index):
         return pl.ds(pl.multiple_of(index * pad, pad), pad)
@@ -130,8 +138,11 @@
 
     slot_col = lax.broadcasted_iota(jnp.int32, (half, cols), 1)
     used = slot_col % pad < vision
-    keep_own = mask_ref[:half, 0:1]
-    keep_prev = mask_ref[:half, 1:2]
+    columns = jnp.concatenate(
+        [jnp.broadcast_to(mask[i:i + 1, :half].astype(jnp.float32), (HD, half)) for i in range(2)],
+        axis=0,
+    ).T
+    keep_own, keep_prev = columns[:, :1], columns[:, HD:HD + 1]
     bias[:, :cols] = jnp.where(used & (keep_own > 0), 0.0, NEGATIVE)
     bias[:, cols:] = jnp.where(used & (keep_prev > 0), 0.0, NEGATIVE)
     live = (keep_own + keep_prev > 0).astype(jnp.float32)
@@ -153,7 +164,7 @@
             [ref[rows, (first + i) * HD:(first + i + 1) * HD] for i in range(group)], axis=0
         )
 
-    def attend(rows, b, first, keys, values, score_bias, live_rows):
+    def attend(rows, b, first, keys, values, score_bias, live_rows, grad_store):
         query = stacked(q, rows, first)
         grad = stacked(do, rows, first)
         scores = dot_nt(query, keys) + score_bias
@@ -165,27 +176,31 @@
         delta = jnp.sum(grad.astype(jnp.float32) * attended, axis=1, keepdims=True)
         grad_weights = dot_nt(grad, values)
         grad_scores = (weights * (grad_weights - delta)).astype(jnp.bfloat16)
-        grad_query = dot(grad_scores, keys) * SCALE
         for i in range(group):
             at = slice((first + i) * HD, (first + i + 1) * HD)
             att[rows, at] = attended[i * half:(i + 1) * half].astype(jnp.bfloat16)
-            gq[rows, at] = grad_query[i * half:(i + 1) * half].astype(jnp.bfloat16)
         to = slice(first * half, (first + group) * half)
+        grad_store[to, :] = grad_scores
         return dot(qt[b, :, to], grad_scores), dot(dot_t[b, :, to], rounded)
 
     def put(b, key_sum, value_sum):
         part[b, :, :HD] = (key_sum * SCALE).T.astype(jnp.bfloat16)
         part[b, :, HD:] = value_sum.T.astype(jnp.bfloat16)
 
-    def write_out(b):
+    def query_grads(rows, grad_store, keys):
+        for first in firsts:
+            grads = dot(grad_store[first * half:(first + group) * half, :], keys) * SCALE
+            for i in range(group):
+                at = slice((first + i) * HD, (first + i + 1) * HD)
+                gq[rows, at] = grads[i * half:(i + 1) * half].astype(jnp.bfloat16)
+
+    stores = []
+
+    def write_out(src, dst, b, k):
         rows = pl.ds(b * half, half)
-        stores = [
-            pltpu.make_async_copy(att.at[rows], att_hbm.at[rows], out_sem.at[b, 0]),
-            pltpu.make_async_copy(gq.at[rows], gq_hbm.at[rows], out_sem.at[b, 1]),
-        ]
-        for store in stores:
-            store.start()
-        return stores
+        store = pltpu.make_async_copy(src.at[rows], dst.at[rows], out_sem.at[b, k])
+        store.start()
+        stores.append(store)
 
     upper, lower = slice(half, tokens), slice(0, half)
     firsts = list(range(0, heads, group))
@@ -195,7 +210,7 @@
     key_sum, value_sum = 0.0, 0.0
     keys, values = kv[0, :, :HD], kv[0, :, HD:]
     for first in firsts[:cut]:
-        key_term, value_term = attend(upper, 1, first, keys, values, own_bias, 1.0)
+        key_term, value_term = attend(upper, 1, first, keys, values, own_bias, 1.0, gs_upper)
         key_sum, value_sum = key_sum + key_term, value_sum + value_term
 
     @pl.when(not_first)
@@ -207,7 +222,9 @@
     both_bias = jnp.concatenate([bias[...]] * group, axis=0)
     key_both, value_both = 0.0, 0.0
     for first in firsts:
-        key_term, value_term = attend(lower, 0, first, both_keys, both_values, both_bias, live)
+        key_term, value_term = attend(
+            lower, 0, first, both_keys, both_values, both_bias, live, gs_lower
+        )
         key_both, value_both = key_both + key_term, value_both + value_term
     put(1, key_both[:, cols:], value_both[:, cols:])
 
@@ -215,15 +232,19 @@
     def _():
         each(n, lambda i: part_copy(1, s - 1, lax.rem(me + i, n), me).start())
 
-    stores = write_out(0)
+    write_out(att, att_hbm, 0, 0)
     key_sum, value_sum = key_sum + key_both[:, :cols], value_sum + value_both[:, :cols]
     for first in firsts[cut:]:
-        key_term, value_term = attend(upper, 1, first, keys, values, own_bias, 1.0)
+        key_term, value_term = attend(upper, 1, first, keys, values, own_bias, 1.0, gs_upper)
         key_sum, value_sum = key_sum + key_term, value_sum + value_term
     put(0, key_sum, value_sum)
     each(n - 1, lambda i: part_copy(0, s, lax.rem(me + 1 + i, n), me).start())
-    stores += write_out(1)
     ret[0, rows_of(me), :] = part[0, rows_of(me), :]
+    write_out(att, att_hbm, 1, 0)
+    query_grads(upper, gs_upper, keys)
+    write_out(gq, gq_hbm, 1, 1)
+    query_grads(lower, gs_lower, both_keys)
+    write_out(gq, gq_hbm, 0, 1)
 
     gather = slot_map(pad, vision, True)
     each(n - 1, lambda i: part_copy(0, s, me, lax.rem(me + 1 + i, n)).wait_recv())
@@ -251,6 +272,15 @@
 
     for store in stores:
         store.wait()
+
+
+def copy_out(*refs):
+    count = len(refs) // 2
+    copies = [pltpu.make_async_copy(refs[i], refs[count + i], refs[-1].at[i]) for i in range(count)]
+    for copy in copies:
+        copy.start()
+    for copy in copies:
+        copy.wait()
 
 
 def per_device(n_seq, n, queries, keys, values, cotangent, mask):
@@ -263,23 +293,28 @@
     cols = n * pad
     bf16, f32 = jnp.bfloat16, jnp.float32
     vmem = pl.BlockSpec(memory_space=pltpu.VMEM)
-    hbm = pl.BlockSpec(memory_space=pl.ANY)
+    hbm = pl.BlockSpec(memory_space=pltpu.HBM)
+    anywhere = pl.BlockSpec(memory_space=pl.ANY)
     dma = pltpu.SemaphoreType.DMA
-    attended, grad_query, grad_keys, grad_values = pl.pallas_call(
+    results = (
+        jax.ShapeDtypeStruct((tokens, width), bf16),
+        jax.ShapeDtypeStruct((tokens, width), bf16),
+        jax.ShapeDtypeStruct((vision * KVH, HD), bf16),
+        jax.ShapeDtypeStruct((vision * KVH, HD), bf16),
+    )
+    found = pl.pallas_call(
         functools.partial(kernel, n_seq, n, pad, vision, group),
-        out_shape=(
-            jax.ShapeDtypeStruct((tokens, width), bf16),
-            jax.ShapeDtypeStruct((tokens, width), bf16),
-            jax.ShapeDtypeStruct((vision * KVH, HD), bf16),
-            jax.ShapeDtypeStruct((vision * KVH, HD), bf16),
-        ),
-        in_specs=[hbm, vmem, vmem, hbm, vmem],
+        out_shape=results,
+        in_specs=[hbm] * 5,
         out_specs=(hbm, hbm, vmem, vmem),
         scratch_shapes=[
             pltpu.VMEM((tokens, width), bf16),
             pltpu.VMEM((tokens, width), bf16),
             pltpu.VMEM((tokens, width), bf16),
             pltpu.VMEM((tokens, width), bf16),
+            pltpu.VMEM((vision * KVH, HD), bf16),
+            pltpu.VMEM((vision * KVH, HD), bf16),
+            pltpu.VMEM((2, tokens), mask.dtype),
             pltpu.VMEM((2, HD, heads * half), bf16),
             pltpu.VMEM((2, HD, heads * half), bf16),
             pltpu.VMEM((KVH * pad, 2 * HD), bf16),
@@ -287,23 +322,34 @@
             pltpu.VMEM((2, cols, 2 * HD), bf16),
             pltpu.VMEM((2, cols, 2 * HD), bf16),
             pltpu.VMEM((half, 2 * cols), f32),
+            pltpu.VMEM((heads * half, 2 * cols), bf16),
+            pltpu.VMEM((heads * half, cols), bf16),
             dma((2, 2)),
             dma((2, 2)),
+            dma((3,)),
             dma((2, n)),
             dma((2, n)),
             dma((2, n)),
             dma((2, n)),
         ],
         compiler_params=pltpu.CompilerParams(
-            collective_id=0, has_side_effects=True, vmem_limit_bytes=48 * 1024 * 1024
+            collective_id=0, has_side_effects=True, vmem_limit_bytes=VMEM_LIMIT
         ),
     )(
         queries,
         keys.reshape(vision * KVH, HD),
         values.reshape(vision * KVH, HD),
         cotangent,
-        mask,
+        mask.T,
     )
+    attended, grad_query, grad_keys, grad_values = pl.pallas_call(
+        copy_out,
+        out_shape=results,
+        in_specs=[anywhere] * 4,
+        out_specs=(hbm,) * 4,
+        scratch_shapes=[dma((4,))],
+        compiler_params=pltpu.CompilerParams(vmem_limit_bytes=VMEM_LIMIT),
+    )(*found)
     shape = (1, vision, KVH, HD)
     return attended, grad_query, grad_keys.reshape(shape), grad_values.reshape(shape)
 

time: 27.9 us -> 57.9 us (2.08)
  Pallas kernels: 20.6 us -> 57.1 us
  local copies, waits for them, and re-layouts: 6.41 us -> 0 us
    pallas_call x0 -> x1, Pallas kernels: none -> 36 us  [per_device(): pl.pallas_call(copy_out, out_shape=results, in_specs=[anywhere] * 4, out_...]
    unnamed x15 -> x0, local copies, waits for them, and re-layouts: 6.41 us -> none
where the time goes in v2:
time: 57.9 us; the launch traced here: 57.7 us
  Pallas kernels  57.1 us (99%)
  between operations  0.64 us (1%)
    pallas_call x1, Pallas kernels, per_device(): pl.pallas_call(copy_out, out_shape=results, in_specs=[anywhere] * 4, out_...  36 us
    pallas_call x1, Pallas kernels, per_device(): pl.pallas_call(functools.partial(kernel, n_seq, n, pad, vision, group), o...  21.1 us

profile of v2, /device:TPU:0, one launch (start us, length us, event | category | flops | bytes accessed | tf_op | source)
XLA Modules:
  0.0 57.7 jit_solution(4546814618469758297)
XLA Ops:
  0.6 21.1 %shard_map.84 = (bf16[256,1024]{1,0:T(8,128)(2,1)}, bf16[256,1024]{1,0:T(8,128)(2,1)}, bf16[200,128]{1,0:T(8,128)(2,1)}, bf16[200,128]{1,0:T(8,128)(2,1)}) custom-call(bf16[256,1024]{1,0:T(8,128)(2,1)} %q_hbm.1, bf16[200,128]{1,0:T(8,128)(2,1)} %bitcast.5, bf16[200,128]{1,0:T(8,128)(2,1)} %bitcast.6, bf16[256,1024]{1,0:T(8,128)(2,1)} %do_hbm.1, s32[2,256]{1,0:T(2,128)} %bitcast.7), custom_call_target="tpu_custom_call" | custom-call | tf_op jit(solution)/shard_map/pallas_call | solution.py:305
  21.7 36.0 %shard_map.85 = (bf16[256,1024]{1,0:T(8,128)(2,1)}, bf16[256,1024]{1,0:T(8,128)(2,1)}, bf16[200,128]{1,0:T(8,128)(2,1)}, bf16[200,128]{1,0:T(8,128)(2,1)}) custom-call(bf16[256,1024]{1,0:T(8,128)(2,1)} %get-tuple-element.12.refs_0_, bf16[256,1024]{1,0:T(8,128)(2,1)} %get-tuple-element.13.refs_1_, bf16[200,128]{1,0:T(8,128)(2,1)} %get-tuple-element.14.refs_2_, ...), custom_call_target="tpu_custom_call" | custom-call | tf_op jit(solution)/shard_map/pallas_call | solution.py:345

commit v3 on v2

--- a/solution.py
+++ b/solution.py
@@ -11,7 +11,7 @@
 KVH = 8
 HD = 128
 NEGATIVE = -1e30
-VMEM_LIMIT = 58 * 1024 * 1024
+VMEM_LIMIT = 53760 * 1024
 MESH = pl.DeviceIdType.MESH
 SCALE = HD ** -0.5
 EXP2_SCALE = SCALE * math.log2(math.e)
@@ -44,9 +44,9 @@
 def kernel(
     n_seq, n, pad, vision, group,
     q_hbm, k_hbm, v_hbm, do_hbm, mask_hbm,
-    att_hbm, gq_hbm, gk_ref, gv_ref,
-    q, do, att, gq, k_own, v_own, mask, qt, dot_t, stage, kv, part, ret, bias, gs_lower, gs_upper,
-    in_sem, out_sem, small_sem, kv_send, kv_recv, part_send, part_recv,
+    att, gq, gk_ref, gv_ref,
+    q, do, k_own, v_own, mask, qt, dot_t, stage, kv, part, ret, bias, gs_lower, gs_upper,
+    in_sem, small_sem, kv_send, kv_recv, part_send, part_recv,
 ):
     s = lax.axis_index("seq")
     me = lax.axis_index("head")
@@ -194,14 +194,6 @@
                 at = slice((first + i) * HD, (first + i + 1) * HD)
                 gq[rows, at] = grads[i * half:(i + 1) * half].astype(jnp.bfloat16)
 
-    stores = []
-
-    def write_out(src, dst, b, k):
-        rows = pl.ds(b * half, half)
-        store = pltpu.make_async_copy(src.at[rows], dst.at[rows], out_sem.at[b, k])
-        store.start()
-        stores.append(store)
-
     upper, lower = slice(half, tokens), slice(0, half)
     firsts = list(range(0, heads, group))
     cut = len(firsts) // 2
@@ -232,7 +224,6 @@
     def _():
         each(n, lambda i: part_copy(1, s - 1, lax.rem(me + i, n), me).start())
 
-    write_out(att, att_hbm, 0, 0)
     key_sum, value_sum = key_sum + key_both[:, :cols], value_sum + value_both[:, :cols]
     for first in firsts[cut:]:
         key_term, value_term = attend(upper, 1, first, keys, values, own_bias, 1.0, gs_upper)
@@ -240,11 +231,8 @@
     put(0, key_sum, value_sum)
     each(n - 1, lambda i: part_copy(0, s, lax.rem(me + 1 + i, n), me).start())
     ret[0, rows_of(me), :] = part[0, rows_of(me), :]
-    write_out(att, att_hbm, 1, 0)
     query_grads(upper, gs_upper, keys)
-    write_out(gq, gq_hbm, 1, 1)
     query_grads(lower, gs_lower, both_keys)
-    write_out(gq, gq_hbm, 0, 1)
 
     gather = slot_map(pad, vision, True)
     each(n - 1, lambda i: part_copy(0, s, me, lax.rem(me + 1 + i, n)).wait_recv())
@@ -269,9 +257,6 @@
     @pl.when(not_first)
     def _():
         each(n, lambda i: part_copy(1, s - 1, lax.rem(me + i, n), me).wait_send())
-
-    for store in stores:
-        store.wait()
 
 
 def copy_out(*refs):
@@ -306,10 +291,8 @@
         functools.partial(kernel, n_seq, n, pad, vision, group),
         out_shape=results,
         in_specs=[hbm] * 5,
-        out_specs=(hbm, hbm, vmem, vmem),
+        out_specs=(vmem,) * 4,
         scratch_shapes=[
-            pltpu.VMEM((tokens, width), bf16),
-            pltpu.VMEM((tokens, width), bf16),
             pltpu.VMEM((tokens, width), bf16),
             pltpu.VMEM((tokens, width), bf16),
             pltpu.VMEM((vision * KVH, HD), bf16),
@@ -324,7 +307,6 @@
             pltpu.VMEM((half, 2 * cols), f32),
             pltpu.VMEM((heads * half, 2 * cols), bf16),
             pltpu.VMEM((heads * half, cols), bf16),
-            dma((2, 2)),
             dma((2, 2)),
             dma((3,)),
             dma((2, n)),
@@ -348,7 +330,6 @@
         in_specs=[anywhere] * 4,
         out_specs=(hbm,) * 4,
         scratch_shapes=[dma((4,))],
-        compiler_params=pltpu.CompilerParams(vmem_limit_bytes=VMEM_LIMIT),
     )(*found)
     shape = (1, vision, KVH, HD)
     return attended, grad_query, grad_keys.reshape(shape), grad_values.reshape(shape)

time: 57.9 us -> 62.5 us (1.079)
  local copies, waits for them, and re-layouts: 0 us -> 5.11 us
    unnamed x0 -> x14, local copies, waits for them, and re-layouts: none -> 5.11 us
where the time goes in v3:
time: 62.5 us; the launch traced here: 62.2 us
  Pallas kernels  56.5 us (90%)
  local copies, waits for them, and re-layouts  5.11 us (8%)
  between operations  0.66 us (1%)
    pallas_call x1, Pallas kernels, per_device(): pl.pallas_call(copy_out, out_shape=results, in_specs=[anywhere] * 4, out_...  36 us
    pallas_call x1, Pallas kernels, per_device(): pl.pallas_call(functools.partial(kernel, n_seq, n, pad, vision, group), o...  20.5 us
    unnamed x14, local copies, waits for them, and re-layouts  5.11 us

profile of v3, /device:TPU:0, one launch (start us, length us, event | category | flops | bytes accessed | tf_op | source)
XLA Modules:
  0.0 62.2 jit_solution(5353590756046475798)
XLA Ops:
  0.6 0.0 copy-start.6
  0.6 0.7 %copy-done.6 = s32[256,2]{0,1:T(2,128)S(1)} copy-done((s32[256,2]{0,1:T(2,128)S(1)}, s32[256,2]{0,1:T(2,128)}, u32[]{:S(2)}) %copy-start.6) | copy-done | bytes 2072
  1.3 0.0 copy-start.2
  1.3 0.8 %copy-done.2 = bf16[1,25,8,128]{3,2,1,0:T(8,128)(2,1)S(1)} copy-done((bf16[1,25,8,128]{3,2,1,0:T(8,128)(2,1)S(1)}, bf16[1,25,8,128]{3,2,1,0:T(8,128)(2,1)}, u32[]{:S(2)}) %copy-start.2) | copy-done | bytes 51224
  2.1 0.0 copy-start.3
  2.1 0.8 %copy-done.3 = bf16[1,25,8,128]{3,2,1,0:T(8,128)(2,1)S(1)} copy-done((bf16[1,25,8,128]{3,2,1,0:T(8,128)(2,1)S(1)}, bf16[1,25,8,128]{3,2,1,0:T(8,128)(2,1)}, u32[]{:S(2)}) %copy-start.3) | copy-done | bytes 51224
  2.9 20.5 %shard_map.84 = (bf16[256,1024]{1,0:T(8,128)(2,1)S(1)}, bf16[256,1024]{1,0:T(8,128)(2,1)S(1)}, bf16[200,128]{1,0:T(8,128)(2,1)S(1)}, bf16[200,128]{1,0:T(8,128)(2,1)S(1)}) custom-call(bf16[256,1024]{1,0:T(8,128)(2,1)} %q_hbm.1, bf16[200,128]{1,0:T(8,128)(2,1)S(1)} %bitcast.5, bf16[200,128]{1,0:T(8,128)(2,1)S(1)} %bitcast.6, bf16[256,1024]{1,0:T(8,128)(2,1)} %do_hbm.1, ...), custom_call_target="tpu_custom_call" | custom-call | tf_op jit(solution)/shard_map/pallas_call | solution.py:290
  23.4 0.0 copy-start
  23.4 0.8 %copy-done = bf16[256,1024]{1,0:T(8,128)(2,1)} copy-done((bf16[256,1024]{1,0:T(8,128)(2,1)}, bf16[256,1024]{1,0:T(8,128)(2,1)S(1)}, u32[]{:S(2)}) %copy-start) | copy-done | bytes 524312
  24.2 0.0 copy-start.1
  24.2 0.8 %copy-done.1 = bf16[256,1024]{1,0:T(8,128)(2,1)} copy-done((bf16[256,1024]{1,0:T(8,128)(2,1)}, bf16[256,1024]{1,0:T(8,128)(2,1)S(1)}, u32[]{:S(2)}) %copy-start.1) | copy-done | bytes 524312
  25.0 0.0 copy-start.4
  25.0 0.6 copy-done.4
  25.6 0.0 copy-start.5
  25.6 0.6 copy-done.5
  26.2 36.0 %shard_map.85 = (bf16[256,1024]{1,0:T(8,128)(2,1)}, bf16[256,1024]{1,0:T(8,128)(2,1)}, bf16[200,128]{1,0:T(8,128)(2,1)}, bf16[200,128]{1,0:T(8,128)(2,1)}) custom-call(bf16[256,1024]{1,0:T(8,128)(2,1)} %copy-done, bf16[256,1024]{1,0:T(8,128)(2,1)} %copy-done.1, bf16[200,128]{1,0:T(8,128)(2,1)} %copy-done.4, bf16[200,128]{1,0:T(8,128)(2,1)} %copy-done.5), custom_call_target="tpu_custom_call" | custom-call | tf_op jit(solution)/shard_map/pallas_call | solution.py:327
Async XLA Ops:
  0.6 0.7 %copy-start.6 = (s32[256,2]{0,1:T(2,128)S(1)}, s32[256,2]{0,1:T(2,128)}, u32[]{:S(2)}) copy-start(s32[256,2]{0,1:T(2,128)} %param.9) | copy-start | bytes 6148
  1.3 0.8 %copy-start.2 = (bf16[1,25,8,128]{3,2,1,0:T(8,128)(2,1)S(1)}, bf16[1,25,8,128]{3,2,1,0:T(8,128)(2,1)}, u32[]{:S(2)}) copy-start(bf16[1,25,8,128]{3,2,1,0:T(8,128)(2,1)} %param.6) | copy-start | bytes 153604
  2.1 0.8 %copy-start.3 = (bf16[1,25,8,128]{3,2,1,0:T(8,128)(2,1)S(1)}, bf16[1,25,8,128]{3,2,1,0:T(8,128)(2,1)}, u32[]{:S(2)}) copy-start(bf16[1,25,8,128]{3,2,1,0:T(8,128)(2,1)} %param.7) | copy-start | bytes 153604
  23.4 0.8 %copy-start = (bf16[256,1024]{1,0:T(8,128)(2,1)}, bf16[256,1024]{1,0:T(8,128)(2,1)S(1)}, u32[]{:S(2)}) copy-start(bf16[256,1024]{1,0:T(8,128)(2,1)S(1)} %get-tuple-element.12.refs_0_) | copy-start | bytes 1572868
  24.2 0.8 %copy-start.1 = (bf16[256,1024]{1,0:T(8,128)(2,1)}, bf16[256,1024]{1,0:T(8,128)(2,1)S(1)}, u32[]{:S(2)}) copy-start(bf16[256,1024]{1,0:T(8,128)(2,1)S(1)} %get-tuple-element.13.refs_1_) | copy-start | bytes 1572868
  25.0 0.6 %copy-start.4 = (bf16[200,128]{1,0:T(8,128)(2,1)}, bf16[200,128]{1,0:T(8,128)(2,1)S(1)}, u32[]{:S(2)}) copy-start(bf16[200,128]{1,0:T(8,128)(2,1)S(1)} %get-tuple-element.14.refs_2_) | copy-start | bytes 153604
  25.6 0.6 copy-start.5

commit v4 on v2

--- a/solution.py
+++ b/solution.py
@@ -275,12 +275,18 @@
 
 
 def copy_out(*refs):
-    count = len(refs) // 2
-    copies = [pltpu.make_async_copy(refs[i], refs[count + i], refs[-1].at[i]) for i in range(count)]
-    for copy in copies:
-        copy.start()
-    for copy in copies:
-        copy.wait()
+    count = (len(refs) - 2) // 3
+    sources, targets, held = refs[:count], refs[count:2 * count], refs[2 * count:3 * count]
+    load_sem, store_sem = refs[3 * count:]
+    loads = [pltpu.make_async_copy(a, b, load_sem.at[i]) for i, (a, b) in enumerate(zip(sources, held))]
+    stores = [pltpu.make_async_copy(a, b, store_sem.at[i]) for i, (a, b) in enumerate(zip(held, targets))]
+    for load in loads:
+        load.start()
+    for load, store in zip(loads, stores):
+        load.wait()
+        store.start()
+    for store in stores:
+        store.wait()
 
 
 def per_device(n_seq, n, queries, keys, values, cotangent, mask):
@@ -288,13 +294,12 @@
     vision = keys.shape[1]
     pad = -(-vision // 16) * 16
     heads = width // HD
-    group = min(2, heads)
+    group = min(4, heads)
     half = tokens // 2
     cols = n * pad
     bf16, f32 = jnp.bfloat16, jnp.float32
     vmem = pl.BlockSpec(memory_space=pltpu.VMEM)
     hbm = pl.BlockSpec(memory_space=pltpu.HBM)
-    anywhere = pl.BlockSpec(memory_space=pl.ANY)
     dma = pltpu.SemaphoreType.DMA
     results = (
         jax.ShapeDtypeStruct((tokens, width), bf16),
@@ -345,9 +350,9 @@
     attended, grad_query, grad_keys, grad_values = pl.pallas_call(
         copy_out,
         out_shape=results,
-        in_specs=[anywhere] * 4,
+        in_specs=[hbm] * 4,
         out_specs=(hbm,) * 4,
-        scratch_shapes=[dma((4,))],
+        scratch_shapes=[pltpu.VMEM(r.shape, bf16) for r in results] + [dma((4,)), dma((4,))],
         compiler_params=pltpu.CompilerParams(vmem_limit_bytes=VMEM_LIMIT),
     )(*found)
     shape = (1, vision, KVH, HD)

time: 57.9 us -> 22.9 us (0.40)
  Pallas kernels: 57.1 us -> 22.1 us
    pallas_call x1, Pallas kernels: 36 us -> 2.09 us  [per_device(): pl.pallas_call(copy_out, out_shape=results, in_specs=[hbm] * 4, out_specs...]
    pallas_call x1, Pallas kernels: 21.1 us -> 20 us  [per_device(): pl.pallas_call(functools.partial(kernel, n_seq, n, pad, vision, group), o...]
where the time goes in v4:
time: 22.9 us; the launch traced here: 22.7 us
  Pallas kernels  22.1 us (97%)
  between operations  0.64 us (3%)
    pallas_call x1, Pallas kernels, per_device(): pl.pallas_call(functools.partial(kernel, n_seq, n, pad, vision, group), o...  20 us
    pallas_call x1, Pallas kernels, per_device(): pl.pallas_call(copy_out, out_shape=results, in_specs=[hbm] * 4, out_specs...  2.09 us

profile of v4, /device:TPU:0, one launch (start us, length us, event | category | flops | bytes accessed | tf_op | source)
XLA Modules:
  0.0 22.7 jit_solution(6364491700941220260)
XLA Ops:
  0.6 20.0 %shard_map.84 = (bf16[256,1024]{1,0:T(8,128)(2,1)}, bf16[256,1024]{1,0:T(8,128)(2,1)}, bf16[200,128]{1,0:T(8,128)(2,1)}, bf16[200,128]{1,0:T(8,128)(2,1)}) custom-call(bf16[256,1024]{1,0:T(8,128)(2,1)} %q_hbm.1, bf16[200,128]{1,0:T(8,128)(2,1)} %bitcast.5, bf16[200,128]{1,0:T(8,128)(2,1)} %bitcast.6, bf16[256,1024]{1,0:T(8,128)(2,1)} %do_hbm.1, s32[2,256]{1,0:T(2,128)} %bitcast.7), custom_call_target="tpu_custom_call" | custom-call | tf_op jit(solution)/shard_map/pallas_call | solution.py:310
  20.6 2.1 %shard_map.85 = (bf16[256,1024]{1,0:T(8,128)(2,1)}, bf16[256,1024]{1,0:T(8,128)(2,1)}, bf16[200,128]{1,0:T(8,128)(2,1)}, bf16[200,128]{1,0:T(8,128)(2,1)}) custom-call(bf16[256,1024]{1,0:T(8,128)(2,1)} %get-tuple-element.12.refs_0_, bf16[256,1024]{1,0:T(8,128)(2,1)} %get-tuple-element.13.refs_1_, bf16[200,128]{1,0:T(8,128)(2,1)} %get-tuple-element.14.refs_2_, ...), custom_call_target="tpu_custom_call" | custom-call | tf_op jit(solution)/shard_map/pallas_call | solution.py:350

commit v5 on v4

--- a/solution.py
+++ b/solution.py
@@ -294,7 +294,7 @@
     vision = keys.shape[1]
     pad = -(-vision // 16) * 16
     heads = width // HD
-    group = min(4, heads)
+    group = min(8, heads)
     half = tokens // 2
     cols = n * pad
     bf16, f32 = jnp.bfloat16, jnp.float32

time: 22.9 us -> 21.9 us (0.956)
  Pallas kernels: 22.1 us -> 21.1 us
    pallas_call x1, Pallas kernels: 20 us -> 19 us  [per_device(): pl.pallas_call(functools.partial(kernel, n_seq, n, pad, vision, group), o...]
where the time goes in v5:
time: 21.9 us; the launch traced here: 21.7 us
  Pallas kernels  21.1 us (96%)
  between operations  0.64 us (3%)
    pallas_call x1, Pallas kernels, per_device(): pl.pallas_call(functools.partial(kernel, n_seq, n, pad, vision, group), o...  19 us
    pallas_call x1, Pallas kernels, per_device(): pl.pallas_call(copy_out, out_shape=results, in_specs=[hbm] * 4, out_specs...  2.09 us

profile of v5, /device:TPU:0, one launch (start us, length us, event | category | flops | bytes accessed | tf_op | source)
XLA Modules:
  0.0 21.7 jit_solution(18309692438754101303)
XLA Ops:
  0.6 19.0 %shard_map.84 = (bf16[256,1024]{1,0:T(8,128)(2,1)}, bf16[256,1024]{1,0:T(8,128)(2,1)}, bf16[200,128]{1,0:T(8,128)(2,1)}, bf16[200,128]{1,0:T(8,128)(2,1)}) custom-call(bf16[256,1024]{1,0:T(8,128)(2,1)} %q_hbm.1, bf16[200,128]{1,0:T(8,128)(2,1)} %bitcast.5, bf16[200,128]{1,0:T(8,128)(2,1)} %bitcast.6, bf16[256,1024]{1,0:T(8,128)(2,1)} %do_hbm.1, s32[2,256]{1,0:T(2,128)} %bitcast.7), custom_call_target="tpu_custom_call" | custom-call | tf_op jit(solution)/shard_map/pallas_call | solution.py:310
  19.6 2.1 %shard_map.85 = (bf16[256,1024]{1,0:T(8,128)(2,1)}, bf16[256,1024]{1,0:T(8,128)(2,1)}, bf16[200,128]{1,0:T(8,128)(2,1)}, bf16[200,128]{1,0:T(8,128)(2,1)}) custom-call(bf16[256,1024]{1,0:T(8,128)(2,1)} %get-tuple-element.12.refs_0_, bf16[256,1024]{1,0:T(8,128)(2,1)} %get-tuple-element.13.refs_1_, bf16[200,128]{1,0:T(8,128)(2,1)} %get-tuple-element.14.refs_2_, ...), custom_call_target="tpu_custom_call" | custom-call | tf_op jit(solution)/shard_map/pallas_call | solution.py:350

commit v6 on v5

--- a/solution.py
+++ b/solution.py
@@ -45,7 +45,7 @@
     n_seq, n, pad, vision, group,
     q_hbm, k_hbm, v_hbm, do_hbm, mask_hbm,
     att_hbm, gq_hbm, gk_ref, gv_ref,
-    q, do, att, gq, k_own, v_own, mask, qt, dot_t, stage, kv, part, ret, bias, gs_lower, gs_upper,
+    q, do, att, gq, k_own, v_own, mask, qt, dot_t, stage, kv, part, ret, bias, w_lower, w_upper, gs_lower, gs_upper,
     in_sem, out_sem, small_sem, kv_send, kv_recv, part_send, part_recv,
 ):
     s = lax.axis_index("seq")
@@ -164,24 +164,29 @@
             [ref[rows, (first + i) * HD:(first + i + 1) * HD] for i in range(group)], axis=0
         )
 
-    def attend(rows, b, first, keys, values, score_bias, live_rows, grad_store):
+    ones = jnp.ones((HD, HD), jnp.bfloat16)
+
+    def attend(rows, first, keys, values, score_bias, live_rows, weight_store, grad_store):
         query = stacked(q, rows, first)
         grad = stacked(do, rows, first)
+        tiles = keys.shape[0] // HD
         scores = dot_nt(query, keys) + score_bias
         peak = jnp.max(scores, axis=1, keepdims=True)
         powered = jnp.exp2((scores - peak) * EXP2_SCALE)
-        weights = powered * (live_rows / jnp.sum(powered, axis=1, keepdims=True))
-        rounded = weights.astype(jnp.bfloat16)
-        attended = dot(rounded, values)
-        delta = jnp.sum(grad.astype(jnp.float32) * attended, axis=1, keepdims=True)
+        beside = jnp.concatenate([values, jnp.ones(values.shape, jnp.bfloat16)], axis=1)
+        sums = dot(powered.astype(jnp.bfloat16), beside)
+        ratio = live_rows / sums[:, HD:]
+        attended = sums[:, :HD] * ratio
+        delta = dot((grad.astype(jnp.float32) * attended).astype(jnp.bfloat16), ones)
+        weights = powered * jnp.concatenate([ratio] * tiles, axis=1)
         grad_weights = dot_nt(grad, values)
-        grad_scores = (weights * (grad_weights - delta)).astype(jnp.bfloat16)
+        grad_scores = weights * (grad_weights - jnp.concatenate([delta] * tiles, axis=1))
         for i in range(group):
             at = slice((first + i) * HD, (first + i + 1) * HD)
             att[rows, at] = attended[i * half:(i + 1) * half].astype(jnp.bfloat16)
         to = slice(first * half, (first + group) * half)
-        grad_store[to, :] = grad_scores
-        return dot(qt[b, :, to], grad_scores), dot(dot_t[b, :, to], rounded)
+        weight_store[to, :] = weights.astype(jnp.bfloat16)
+        grad_store[to, :] = grad_scores.astype(jnp.bfloat16)
 
     def put(b, key_sum, value_sum):
         part[b, :, :HD] = (key_sum * SCALE).T.astype(jnp.bfloat16)
@@ -204,14 +209,8 @@
 
     upper, lower = slice(half, tokens), slice(0, half)
     firsts = list(range(0, heads, group))
-    cut = len(firsts) // 2
 
     each(n - 1, lambda i: kv_copy(0, s, me, lax.rem(me + 1 + i, n)).wait_recv())
-    key_sum, value_sum = 0.0, 0.0
-    keys, values = kv[0, :, :HD], kv[0, :, HD:]
-    for first in firsts[:cut]:
-        key_term, value_term = attend(upper, 1, first, keys, values, own_bias, 1.0, gs_upper)
-        key_sum, value_sum = key_sum + key_term, value_sum + value_term
 
     @pl.when(not_first)
     def _():
@@ -220,24 +219,23 @@
     both_keys = kv[:, :, :HD].reshape(2 * cols, HD)
     both_values = kv[:, :, HD:].reshape(2 * cols, HD)
     both_bias = jnp.concatenate([bias[...]] * group, axis=0)
-    key_both, value_both = 0.0, 0.0
     for first in firsts:
-        key_term, value_term = attend(
-            lower, 0, first, both_keys, both_values, both_bias, live, gs_lower
-        )
-        key_both, value_both = key_both + key_term, value_both + value_term
-    put(1, key_both[:, cols:], value_both[:, cols:])
+        attend(lower, first, both_keys, both_values, both_bias, live, w_lower, gs_lower)
+    put(1, dot(qt[0], gs_lower[:, cols:]), dot(dot_t[0], w_lower[:, cols:]))
 
     @pl.when(not_first)
     def _():
         each(n, lambda i: part_copy(1, s - 1, lax.rem(me + i, n), me).start())
 
     write_out(att, att_hbm, 0, 0)
-    key_sum, value_sum = key_sum + key_both[:, :cols], value_sum + value_both[:, :cols]
-    for first in firsts[cut:]:
-        key_term, value_term = attend(upper, 1, first, keys, values, own_bias, 1.0, gs_upper)
-        key_sum, value_sum = key_sum + key_term, value_sum + value_term
-    put(0, key_sum, value_sum)
+    keys, values = kv[0, :, :HD], kv[0, :, HD:]
+    for first in firsts:
+        attend(upper, first, keys, values, own_bias, 1.0, w_upper, gs_upper)
+    put(
+        0,
+        dot(qt[0], gs_lower[:, :cols]) + dot(qt[1], gs_upper[...]),
+        dot(dot_t[0], w_lower[:, :cols]) + dot(dot_t[1], w_upper[...]),
+    )
     each(n - 1, lambda i: part_copy(0, s, lax.rem(me + 1 + i, n), me).start())
     ret[0, rows_of(me), :] = part[0, rows_of(me), :]
     write_out(att, att_hbm, 1, 0)
@@ -274,12 +272,22 @@
         store.wait()
 
 
-def copy_out(*refs):
+def copy_out(pieces, *refs):
     count = (len(refs) - 2) // 3
     sources, targets, held = refs[:count], refs[count:2 * count], refs[2 * count:3 * count]
     load_sem, store_sem = refs[3 * count:]
-    loads = [pltpu.make_async_copy(a, b, load_sem.at[i]) for i, (a, b) in enumerate(zip(sources, held))]
-    stores = [pltpu.make_async_copy(a, b, store_sem.at[i]) for i, (a, b) in enumerate(zip(held, targets))]
+    loads, stores = [], []
+    for source, target, buffer, cut in zip(sources, targets, held, pieces):
+        size = source.shape[0] // cut
+        for i in range(cut):
+            rows = pl.ds(i * size, size)
+            at = len(loads)
+            loads.append(
+                pltpu.make_async_copy(source.at[rows], buffer.at[rows], load_sem.at[at])
+            )
+            stores.append(
+                pltpu.make_async_copy(buffer.at[rows], target.at[rows], store_sem.at[at])
+            )
     for load in loads:
         load.start()
     for load, store in zip(loads, stores):
@@ -301,6 +309,7 @@
     vmem = pl.BlockSpec(memory_space=pltpu.VMEM)
     hbm = pl.BlockSpec(memory_space=pltpu.HBM)
     dma = pltpu.SemaphoreType.DMA
+    pieces = (4, 4, 1, 1)
     results = (
         jax.ShapeDtypeStruct((tokens, width), bf16),
         jax.ShapeDtypeStruct((tokens, width), bf16),
@@ -329,6 +338,8 @@
             pltpu.VMEM((half, 2 * cols), f32),
             pltpu.VMEM((heads * half, 2 * cols), bf16),
             pltpu.VMEM((heads * half, cols), bf16),
+            pltpu.VMEM((heads * half, 2 * cols), bf16),
+            pltpu.VMEM((heads * half, cols), bf16),
             dma((2, 2)),
             dma((2, 2)),
             dma((3,)),
@@ -348,11 +359,11 @@
         mask.T,
     )
     attended, grad_query, grad_keys, grad_values = pl.pallas_call(
-        copy_out,
+        functools.partial(copy_out, pieces),
         out_shape=results,
         in_specs=[hbm] * 4,
         out_specs=(hbm,) * 4,
-        scratch_shapes=[pltpu.VMEM(r.shape, bf16) for r in results] + [dma((4,)), dma((4,))],
+        scratch_shapes=[pltpu.VMEM(r.shape, bf16) for r in results] + [dma((sum(pieces),))] * 2,
         compiler_params=pltpu.CompilerParams(vmem_limit_bytes=VMEM_LIMIT),
     )(*found)
     shape = (1, vision, KVH, HD)

time: 21.9 us -> 21.8 us (level)
  no operation moved by 1% of the time
where the time goes in v6:
time: 21.8 us; the launch traced here: 21.6 us
  Pallas kernels  21 us (96%)
  between operations  0.64 us (3%)
    pallas_call x1, Pallas kernels, per_device(): pl.pallas_call(functools.partial(kernel, n_seq, n, pad, vision, group), o...  18.8 us
    pallas_call x1, Pallas kernels, per_device(): pl.pallas_call(functools.partial(copy_out, pieces), out_shape=results, in...  2.15 us

profile of v6, /device:TPU:0, one launch (start us, length us, event | category | flops | bytes accessed | tf_op | source)
XLA Modules:
  0.0 21.6 jit_solution(3800912632995257613)
XLA Ops:
  0.6 18.8 %shard_map.84 = (bf16[256,1024]{1,0:T(8,128)(2,1)}, bf16[256,1024]{1,0:T(8,128)(2,1)}, bf16[200,128]{1,0:T(8,128)(2,1)}, bf16[200,128]{1,0:T(8,128)(2,1)}) custom-call(bf16[256,1024]{1,0:T(8,128)(2,1)} %q_hbm.1, bf16[200,128]{1,0:T(8,128)(2,1)} %bitcast.5, bf16[200,128]{1,0:T(8,128)(2,1)} %bitcast.6, bf16[256,1024]{1,0:T(8,128)(2,1)} %do_hbm.1, s32[2,256]{1,0:T(2,128)} %bitcast.7), custom_call_target="tpu_custom_call" | custom-call | tf_op jit(solution)/shard_map/pallas_call | solution.py:319
  19.5 2.1 %shard_map.85 = (bf16[256,1024]{1,0:T(8,128)(2,1)}, bf16[256,1024]{1,0:T(8,128)(2,1)}, bf16[200,128]{1,0:T(8,128)(2,1)}, bf16[200,128]{1,0:T(8,128)(2,1)}) custom-call(bf16[256,1024]{1,0:T(8,128)(2,1)} %get-tuple-element.12.refs_0_, bf16[256,1024]{1,0:T(8,128)(2,1)} %get-tuple-element.13.refs_1_, bf16[200,128]{1,0:T(8,128)(2,1)} %get-tuple-element.14.refs_2_, ...), custom_call_target="tpu_custom_call" | custom-call | tf_op jit(solution)/shard_map/pallas_call | solution.py:361

commit v7 on v6

--- a/solution.py
+++ b/solution.py
@@ -171,15 +171,18 @@
         grad = stacked(do, rows, first)
         tiles = keys.shape[0] // HD
         scores = dot_nt(query, keys) + score_bias
+        yield
+        grad_weights = dot_nt(grad, values)
         peak = jnp.max(scores, axis=1, keepdims=True)
         powered = jnp.exp2((scores - peak) * EXP2_SCALE)
+        yield
         beside = jnp.concatenate([values, jnp.ones(values.shape, jnp.bfloat16)], axis=1)
         sums = dot(powered.astype(jnp.bfloat16), beside)
         ratio = live_rows / sums[:, HD:]
         attended = sums[:, :HD] * ratio
         delta = dot((grad.astype(jnp.float32) * attended).astype(jnp.bfloat16), ones)
+        yield
         weights = powered * jnp.concatenate([ratio] * tiles, axis=1)
-        grad_weights = dot_nt(grad, values)
         grad_scores = weights * (grad_weights - jnp.concatenate([delta] * tiles, axis=1))
         for i in range(group):
             at = slice((first + i) * HD, (first + i + 1) * HD)
@@ -187,6 +190,14 @@
         to = slice(first * half, (first + group) * half)
         weight_store[to, :] = weights.astype(jnp.bfloat16)
         grad_store[to, :] = grad_scores.astype(jnp.bfloat16)
+        yield
+
+    def in_step(chunks):
+        stages = 4
+        for time in range(stages + len(chunks) - 1):
+            for place in reversed(range(len(chunks))):
+                if 0 <= time - place < stages:
+                    next(chunks[place])
 
     def put(b, key_sum, value_sum):
         part[b, :, :HD] = (key_sum * SCALE).T.astype(jnp.bfloat16)
@@ -219,8 +230,10 @@
     both_keys = kv[:, :, :HD].reshape(2 * cols, HD)
     both_values = kv[:, :, HD:].reshape(2 * cols, HD)
     both_bias = jnp.concatenate([bias[...]] * group, axis=0)
-    for first in firsts:
+    in_step([
         attend(lower, first, both_keys, both_values, both_bias, live, w_lower, gs_lower)
+        for first in firsts
+    ])
     put(1, dot(qt[0], gs_lower[:, cols:]), dot(dot_t[0], w_lower[:, cols:]))
 
     @pl.when(not_first)
@@ -229,8 +242,9 @@
 
     write_out(att, att_hbm, 0, 0)
     keys, values = kv[0, :, :HD], kv[0, :, HD:]
-    for first in firsts:
-        attend(upper, first, keys, values, own_bias, 1.0, w_upper, gs_upper)
+    in_step([
+        attend(upper, first, keys, values, own_bias, 1.0, w_upper, gs_upper) for first in firsts
+    ])
     put(
         0,
         dot(qt[0], gs_lower[:, :cols]) + dot(qt[1], gs_upper[...]),
@@ -302,14 +316,14 @@
     vision = keys.shape[1]
     pad = -(-vision // 16) * 16
     heads = width // HD
-    group = min(8, heads)
+    group = min(4, heads)
     half = tokens // 2
     cols = n * pad
     bf16, f32 = jnp.bfloat16, jnp.float32
     vmem = pl.BlockSpec(memory_space=pltpu.VMEM)
     hbm = pl.BlockSpec(memory_space=pltpu.HBM)
     dma = pltpu.SemaphoreType.DMA
-    pieces = (4, 4, 1, 1)
+    pieces = (1, 1, 1, 1)
     results = (
         jax.ShapeDtypeStruct((tokens, width), bf16),
         jax.ShapeDtypeStruct((tokens, width), bf16),

time: 21.8 us -> 21.5 us (0.986)
  Pallas kernels: 21 us -> 20.7 us
where the time goes in v7:
time: 21.5 us; the launch traced here: 21.4 us
  Pallas kernels  20.7 us (96%)
  between operations  0.64 us (3%)
    pallas_call x1, Pallas kernels, per_device(): pl.pallas_call(functools.partial(kernel, n_seq, n, pad, vision, group), o...  18.6 us
    pallas_call x1, Pallas kernels, per_device(): pl.pallas_call(functools.partial(copy_out, pieces), out_shape=results, in...  2.09 us

profile of v7, /device:TPU:0, one launch (start us, length us, event | category | flops | bytes accessed | tf_op | source)
XLA Modules:
  0.0 21.4 jit_solution(9804832108136193662)
XLA Ops:
  0.6 18.6 %shard_map.84 = (bf16[256,1024]{1,0:T(8,128)(2,1)}, bf16[256,1024]{1,0:T(8,128)(2,1)}, bf16[200,128]{1,0:T(8,128)(2,1)}, bf16[200,128]{1,0:T(8,128)(2,1)}) custom-call(bf16[256,1024]{1,0:T(8,128)(2,1)} %q_hbm.1, bf16[200,128]{1,0:T(8,128)(2,1)} %bitcast.5, bf16[200,128]{1,0:T(8,128)(2,1)} %bitcast.6, bf16[256,1024]{1,0:T(8,128)(2,1)} %do_hbm.1, s32[2,256]{1,0:T(2,128)} %bitcast.7), custom_call_target="tpu_custom_call" | custom-call | tf_op jit(solution)/shard_map/pallas_call | solution.py:333
  19.3 2.1 %shard_map.85 = (bf16[256,1024]{1,0:T(8,128)(2,1)}, bf16[256,1024]{1,0:T(8,128)(2,1)}, bf16[200,128]{1,0:T(8,128)(2,1)}, bf16[200,128]{1,0:T(8,128)(2,1)}) custom-call(bf16[256,1024]{1,0:T(8,128)(2,1)} %get-tuple-element.12.refs_0_, bf16[256,1024]{1,0:T(8,128)(2,1)} %get-tuple-element.13.refs_1_, bf16[200,128]{1,0:T(8,128)(2,1)} %get-tuple-element.14.refs_2_, ...), custom_call_target="tpu_custom_call" | custom-call | tf_op jit(solution)/shard_map/pallas_call | solution.py:375

commit v8 on v7

--- a/solution.py
+++ b/solution.py
@@ -44,9 +44,9 @@
 def kernel(
     n_seq, n, pad, vision, group,
     q_hbm, k_hbm, v_hbm, do_hbm, mask_hbm,
-    att_hbm, gq_hbm, gk_ref, gv_ref,
-    q, do, att, gq, k_own, v_own, mask, qt, dot_t, stage, kv, part, ret, bias, w_lower, w_upper, gs_lower, gs_upper,
-    in_sem, out_sem, small_sem, kv_send, kv_recv, part_send, part_recv,
+    att_hbm, gq_hbm, ret,
+    q, do, att, gq, k_own, v_own, mask, qt, dot_t, stage, kv, part, bias, w_lower, w_upper, gs_lower, gs_upper,
+    in_sem, out_sem, small_sem, kv_send, kv_recv, part_send, part_recv, kept_sem,
 ):
     s = lax.axis_index("seq")
     me = lax.axis_index("head")
@@ -120,21 +120,17 @@
         barrier, (n - 1) + n * not_first.astype(jnp.int32) + n * not_last.astype(jnp.int32)
     )
 
+
+    @pl.when(not_last)
+    def _():
+        each(n, lambda i: kv_copy(1, s + 1, lax.rem(me + i, n), me).start())
+
     each(n - 1, lambda i: kv_copy(0, s, lax.rem(me + 1 + i, n), me).start())
-
-    @pl.when(not_last)
-    def _():
-        each(n, lambda i: kv_copy(1, s + 1, lax.rem(me + i, n), me).start())
-
     kv[0, rows_of(me), :] = stage[rows_of(me // copies), :]
 
     @pl.when(s == 0)
     def _():
         kv[1] = jnp.zeros(kv.shape[1:], kv.dtype)
-
-    @pl.when(s == n_seq - 1)
-    def _():
-        ret[1] = jnp.zeros(ret.shape[1:], ret.dtype)
 
     slot_col = lax.broadcasted_iota(jnp.int32, (half, cols), 1)
     used = slot_col % pad < vision
@@ -251,26 +247,21 @@
         dot(dot_t[0], w_lower[:, :cols]) + dot(dot_t[1], w_upper[...]),
     )
     each(n - 1, lambda i: part_copy(0, s, lax.rem(me + 1 + i, n), me).start())
-    ret[0, rows_of(me), :] = part[0, rows_of(me), :]
+    kept = pltpu.make_async_copy(part.at[0, rows_of(me)], ret.at[0, rows_of(me)], kept_sem)
+    kept.start()
     write_out(att, att_hbm, 1, 0)
     query_grads(upper, gs_upper, keys)
     write_out(gq, gq_hbm, 1, 1)
     query_grads(lower, gs_lower, both_keys)
     write_out(gq, gq_hbm, 0, 1)
 
-    gather = slot_map(pad, vision, True)
     each(n - 1, lambda i: part_copy(0, s, me, lax.rem(me + 1 + i, n)).wait_recv())
 
     @pl.when(not_last)
     def _():
         each(n, lambda i: part_copy(1, s, me, lax.rem(me + i, n)).wait_recv())
 
-    total = ret[0].astype(jnp.float32) + ret[1].astype(jnp.float32)
-    total = total.reshape(KVH, copies, pad, 2 * HD).sum(axis=1).reshape(KVH * pad, 2 * HD)
-    grads = dot(gather, total.astype(jnp.bfloat16)).astype(jnp.bfloat16)
-    gk_ref[...] = grads[:, :HD]
-    gv_ref[...] = grads[:, HD:]
-
+    kept.wait()
     each(n - 1, lambda i: kv_copy(0, s, lax.rem(me + 1 + i, n), me).wait_send())
     each(n - 1, lambda i: part_copy(0, s, lax.rem(me + 1 + i, n), me).wait_send())
 
@@ -286,27 +277,40 @@
         store.wait()
 
 
-def copy_out(pieces, *refs):
-    count = (len(refs) - 2) // 3
-    sources, targets, held = refs[:count], refs[count:2 * count], refs[2 * count:3 * count]
-    load_sem, store_sem = refs[3 * count:]
+def finish(
+    n_seq, pad, vision, att_in, gq_in, ret_in, att_out, gq_out, gk_out, gv_out,
+    att, gq, ret, gk, gv, load_sem, store_sem,
+):
+    not_last = lax.axis_index("seq") < n_seq - 1
+    own = pltpu.make_async_copy(ret_in.at[0], ret.at[0], load_sem.at[0])
+    following = pltpu.make_async_copy(ret_in.at[1], ret.at[1], load_sem.at[1])
+    own.start()
+    pl.when(not_last)(following.start)
     loads, stores = [], []
-    for source, target, buffer, cut in zip(sources, targets, held, pieces):
-        size = source.shape[0] // cut
-        for i in range(cut):
-            rows = pl.ds(i * size, size)
-            at = len(loads)
-            loads.append(
-                pltpu.make_async_copy(source.at[rows], buffer.at[rows], load_sem.at[at])
-            )
-            stores.append(
-                pltpu.make_async_copy(buffer.at[rows], target.at[rows], store_sem.at[at])
-            )
+    for i, (source, buffer, target) in enumerate(((att_in, att, att_out), (gq_in, gq, gq_out))):
+        loads.append(pltpu.make_async_copy(source, buffer, load_sem.at[2 + i]))
+        stores.append(pltpu.make_async_copy(buffer, target, store_sem.at[i]))
     for load in loads:
         load.start()
+
+    @pl.when(jnp.logical_not(not_last))
+    def _():
+        ret[1] = jnp.zeros(ret.shape[1:], ret.dtype)
+
+    gather = slot_map(pad, vision, True)
+    own.wait()
+    pl.when(not_last)(following.wait)
     for load, store in zip(loads, stores):
         load.wait()
         store.start()
+    total = ret[0].astype(jnp.float32) + ret[1].astype(jnp.float32)
+    copies = ret.shape[1] // (KVH * pad)
+    total = total.reshape(KVH, copies, pad, 2 * HD).sum(axis=1).reshape(KVH * pad, 2 * HD)
+    grads = dot(gather, total.astype(jnp.bfloat16)).astype(jnp.bfloat16)
+    for i, (buffer, target) in enumerate(((gk, gk_out), (gv, gv_out))):
+        buffer[...] = grads[:, i * HD:(i + 1) * HD]
+        stores.append(pltpu.make_async_copy(buffer, target, store_sem.at[2 + i]))
+        stores[-1].start()
     for store in stores:
         store.wait()
 
@@ -320,10 +324,8 @@
     half = tokens // 2
     cols = n * pad
     bf16, f32 = jnp.bfloat16, jnp.float32
-    vmem = pl.BlockSpec(memory_space=pltpu.VMEM)
     hbm = pl.BlockSpec(memory_space=pltpu.HBM)
     dma = pltpu.SemaphoreType.DMA
-    pieces = (1, 1, 1, 1)
     results = (
         jax.ShapeDtypeStruct((tokens, width), bf16),
         jax.ShapeDtypeStruct((tokens, width), bf16),
@@ -332,9 +334,9 @@
     )
     found = pl.pallas_call(
         functools.partial(kernel, n_seq, n, pad, vision, group),
-        out_shape=results,
+        out_shape=results[:2] + (jax.ShapeDtypeStruct((2, cols, 2 * HD), bf16),),
         in_specs=[hbm] * 5,
-        out_specs=(hbm, hbm, vmem, vmem),
+        out_specs=(hbm,) * 3,
         scratch_shapes=[
             pltpu.VMEM((tokens, width), bf16),
             pltpu.VMEM((tokens, width), bf16),
@@ -346,7 +348,6 @@
             pltpu.VMEM((2, HD, heads * half), bf16),
             pltpu.VMEM((2, HD, heads * half), bf16),
             pltpu.VMEM((KVH * pad, 2 * HD), bf16),
-            pltpu.VMEM((2, cols, 2 * HD), bf16),
             pltpu.VMEM((2, cols, 2 * HD), bf16),
             pltpu.VMEM((2, cols, 2 * HD), bf16),
             pltpu.VMEM((half, 2 * cols), f32),
@@ -361,6 +362,7 @@
             dma((2, n)),
             dma((2, n)),
             dma((2, n)),
+            dma,
         ],
         compiler_params=pltpu.CompilerParams(
             collective_id=0, has_side_effects=True, vmem_limit_bytes=VMEM_LIMIT
@@ -373,11 +375,19 @@
         mask.T,
     )
     attended, grad_query, grad_keys, grad_values = pl.pallas_call(
-        functools.partial(copy_out, pieces),
+        functools.partial(finish, n_seq, pad, vision),
         out_shape=results,
-        in_specs=[hbm] * 4,
+        in_specs=[hbm] * 3,
         out_specs=(hbm,) * 4,
-        scratch_shapes=[pltpu.VMEM(r.shape, bf16) for r in results] + [dma((sum(pieces),))] * 2,
+        scratch_shapes=[
+            pltpu.VMEM((tokens, width), bf16),
+            pltpu.VMEM((tokens, width), bf16),
+            pltpu.VMEM((2, cols, 2 * HD), bf16),
+            pltpu.VMEM((vision * KVH, HD), bf16),
+            pltpu.VMEM((vision * KVH, HD), bf16),
+            dma((4,)),
+            dma((4,)),
+        ],
         compiler_params=pltpu.CompilerParams(vmem_limit_bytes=VMEM_LIMIT),
     )(*found)
     shape = (1, vision, KVH, HD)

time: 21.5 us -> 20.9 us (0.972)
  Pallas kernels: 20.7 us -> 20.1 us
    pallas_call x1, Pallas kernels: 18.6 us -> 17.9 us  [per_device(): pl.pallas_call(functools.partial(kernel, n_seq, n, pad, vision, group), o...]
where the time goes in v8:
time: 20.9 us; the launch traced here: 20.8 us
  Pallas kernels  20.1 us (96%)
  between operations  0.64 us (3%)
    pallas_call x1, Pallas kernels, per_device(): pl.pallas_call(functools.partial(kernel, n_seq, n, pad, vision, group), o...  17.9 us
    pallas_call x1, Pallas kernels, per_device(): pl.pallas_call(functools.partial(finish, n_seq, pad, vision), out_shape=r...  2.24 us

profile of v8, /device:TPU:0, one launch (start us, length us, event | category | flops | bytes accessed | tf_op | source)
XLA Modules:
  0.0 20.8 jit_solution(14886870076122948474)
XLA Ops:
  0.6 17.9 %shard_map.84 = (bf16[256,1024]{1,0:T(8,128)(2,1)}, bf16[256,1024]{1,0:T(8,128)(2,1)}, bf16[2,256,256]{2,1,0:T(8,128)(2,1)}) custom-call(bf16[256,1024]{1,0:T(8,128)(2,1)} %q_hbm.1, bf16[200,128]{1,0:T(8,128)(2,1)} %bitcast.5, bf16[200,128]{1,0:T(8,128)(2,1)} %bitcast.6, bf16[256,1024]{1,0:T(8,128)(2,1)} %do_hbm.1, s32[2,256]{1,0:T(2,128)} %bitcast.7), custom_call_target="tpu_custom_call" | custom-call | tf_op jit(solution)/shard_map/pallas_call | solution.py:335
  18.5 2.2 %shard_map.85 = (bf16[256,1024]{1,0:T(8,128)(2,1)}, bf16[256,1024]{1,0:T(8,128)(2,1)}, bf16[200,128]{1,0:T(8,128)(2,1)}, bf16[200,128]{1,0:T(8,128)(2,1)}) custom-call(bf16[256,1024]{1,0:T(8,128)(2,1)} %get-tuple-element.11.att_in, bf16[256,1024]{1,0:T(8,128)(2,1)} %get-tuple-element.12.gq_in, bf16[2,256,256]{2,1,0:T(8,128)(2,1)} %get-tuple-element.13.ret_in), custom_call_target="tpu_custom_call" | custom-call | tf_op jit(solution)/shard_map/pallas_call | solution.py:377

commit v9 on v8

--- a/solution.py
+++ b/solution.py
@@ -147,13 +147,16 @@
 
     for load in loads:
         load.wait()
-    for h in range(heads):
-        at = slice(h * HD, (h + 1) * HD)
-        for b in range(2):
+
+    def turn(b):
+        for h in range(heads):
+            at = slice(h * HD, (h + 1) * HD)
             to = slice(h * half, (h + 1) * half)
             rows = slice(b * half, (b + 1) * half)
             qt[b, :, to] = q[rows, at].T
             dot_t[b, :, to] = do[rows, at].T
+
+    turn(0)
 
     def stacked(ref, rows, first):
         return jnp.concatenate(
@@ -196,8 +199,8 @@
                     next(chunks[place])
 
     def put(b, key_sum, value_sum):
-        part[b, :, :HD] = (key_sum * SCALE).T.astype(jnp.bfloat16)
-        part[b, :, HD:] = value_sum.T.astype(jnp.bfloat16)
+        part[b, :, :HD] = (key_sum * SCALE).astype(jnp.bfloat16).T
+        part[b, :, HD:] = value_sum.astype(jnp.bfloat16).T
 
     def query_grads(rows, grad_store, keys):
         for first in firsts:
@@ -237,6 +240,7 @@
         each(n, lambda i: part_copy(1, s - 1, lax.rem(me + i, n), me).start())
 
     write_out(att, att_hbm, 0, 0)
+    turn(1)
     keys, values = kv[0, :, :HD], kv[0, :, HD:]
     in_step([
         attend(upper, first, keys, values, own_bias, 1.0, w_upper, gs_upper) for first in firsts

time: 20.9 us -> 21 us (level)
  no operation moved by 1% of the time
where the time goes in v9:
time: 21 us; the launch traced here: 20.8 us
  Pallas kernels  20.1 us (96%)
  between operations  0.64 us (3%)
    pallas_call x1, Pallas kernels, per_device(): pl.pallas_call(functools.partial(kernel, n_seq, n, pad, vision, group), o...  17.9 us
    pallas_call x1, Pallas kernels, per_device(): pl.pallas_call(functools.partial(finish, n_seq, pad, vision), out_shape=r...  2.24 us

profile of v9, /device:TPU:0, one launch (start us, length us, event | category | flops | bytes accessed | tf_op | source)
XLA Modules:
  0.0 20.8 jit_solution(11817688323952072367)
XLA Ops:
  0.6 17.9 %shard_map.84 = (bf16[256,1024]{1,0:T(8,128)(2,1)}, bf16[256,1024]{1,0:T(8,128)(2,1)}, bf16[2,256,256]{2,1,0:T(8,128)(2,1)}) custom-call(bf16[256,1024]{1,0:T(8,128)(2,1)} %q_hbm.1, bf16[200,128]{1,0:T(8,128)(2,1)} %bitcast.5, bf16[200,128]{1,0:T(8,128)(2,1)} %bitcast.6, bf16[256,1024]{1,0:T(8,128)(2,1)} %do_hbm.1, s32[2,256]{1,0:T(2,128)} %bitcast.7), custom_call_target="tpu_custom_call" | custom-call | tf_op jit(solution)/shard_map/pallas_call | solution.py:339
  18.6 2.2 %shard_map.85 = (bf16[256,1024]{1,0:T(8,128)(2,1)}, bf16[256,1024]{1,0:T(8,128)(2,1)}, bf16[200,128]{1,0:T(8,128)(2,1)}, bf16[200,128]{1,0:T(8,128)(2,1)}) custom-call(bf16[256,1024]{1,0:T(8,128)(2,1)} %get-tuple-element.11.att_in, bf16[256,1024]{1,0:T(8,128)(2,1)} %get-tuple-element.12.gq_in, bf16[2,256,256]{2,1,0:T(8,128)(2,1)} %get-tuple-element.13.ret_in), custom_call_target="tpu_custom_call" | custom-call | tf_op jit(solution)/shard_map/pallas_call | solution.py:381

commit v10 on v8

--- a/solution.py
+++ b/solution.py
@@ -320,7 +320,7 @@
     vision = keys.shape[1]
     pad = -(-vision // 16) * 16
     heads = width // HD
-    group = min(4, heads)
+    group = min(8, heads)
     half = tokens // 2
     cols = n * pad
     bf16, f32 = jnp.bfloat16, jnp.float32

time: 20.9 us -> 21.1 us (level)
  no operation moved by 1% of the time
where the time goes in v10:
time: 21.1 us; the launch traced here: 20.9 us
  Pallas kernels  20.3 us (96%)
  between operations  0.64 us (3%)
    pallas_call x1, Pallas kernels, per_device(): pl.pallas_call(functools.partial(kernel, n_seq, n, pad, vision, group), o...  18.1 us
    pallas_call x1, Pallas kernels, per_device(): pl.pallas_call(functools.partial(finish, n_seq, pad, vision), out_shape=r...  2.23 us

profile of v10, /device:TPU:0, one launch (start us, length us, event | category | flops | bytes accessed | tf_op | source)
XLA Modules:
  0.0 20.9 jit_solution(12956130380967155362)
XLA Ops:
  0.6 18.1 %shard_map.84 = (bf16[256,1024]{1,0:T(8,128)(2,1)}, bf16[256,1024]{1,0:T(8,128)(2,1)}, bf16[2,256,256]{2,1,0:T(8,128)(2,1)}) custom-call(bf16[256,1024]{1,0:T(8,128)(2,1)} %q_hbm.1, bf16[200,128]{1,0:T(8,128)(2,1)} %bitcast.5, bf16[200,128]{1,0:T(8,128)(2,1)} %bitcast.6, bf16[256,1024]{1,0:T(8,128)(2,1)} %do_hbm.1, s32[2,256]{1,0:T(2,128)} %bitcast.7), custom_call_target="tpu_custom_call" | custom-call | tf_op jit(solution)/shard_map/pallas_call | solution.py:335
  18.7 2.2 %shard_map.85 = (bf16[256,1024]{1,0:T(8,128)(2,1)}, bf16[256,1024]{1,0:T(8,128)(2,1)}, bf16[200,128]{1,0:T(8,128)(2,1)}, bf16[200,128]{1,0:T(8,128)(2,1)}) custom-call(bf16[256,1024]{1,0:T(8,128)(2,1)} %get-tuple-element.11.att_in, bf16[256,1024]{1,0:T(8,128)(2,1)} %get-tuple-element.12.gq_in, bf16[2,256,256]{2,1,0:T(8,128)(2,1)} %get-tuple-element.13.ret_in), custom_call_target="tpu_custom_call" | custom-call | tf_op jit(solution)/shard_map/pallas_call | solution.py:377
